TPU v7x, 512 devices: a whole 4x8x8 slice. The times are simulated.
512 devices in a mesh: fsdp: 32 (over y_hi, x, core), tensor: 16 (over y_lo, z).
Axes of the slice: x: 4, y: 8 (y_hi: 4, y_lo: 2; y = y_hi * 2 + y_lo), z: 8, core: 2. Of those that a mesh axis runs over, the one named last changes fastest.
Arguments:
- moment: bfloat16 [4096, 12800], P('fsdp', 'tensor'), may hold values from -4.5 to 4.5
Outputs:
- updated: bfloat16 [4096, 12800], P('fsdp', 'tensor')
All inputs are finite; a program needn't handle non-finite values.
Results may differ from a plain program's by a relative error of at most 0.0097.
Values may be sent and summed in bfloat16 or wider, within the bound.
No kernel may reach another device: no remote copies, remote signals or barrier semaphores. Data moves between devices by JAX's collectives and lax.ppermute only.
A program may use at most 64 MiB of HBM per device.

v0:
```python
import jax
import jax.numpy as jnp
from jax import lax
from jax.sharding import PartitionSpec as P

COLS = 12800


coef_linear = 3.4445
coef_cubic = -4.775
coef_quintic = 2.0315


def panel_product(matrix, piece):
    return jnp.dot(matrix, piece, preferred_element_type=jnp.float32)


def on_device(moment):
    contract = (((1,), (1,)), ((), ()))
    everyone = lax.all_gather(moment, "fsdp", axis=0, tiled=True)
    partial_value = lax.dot_general(moment, everyone, contract, preferred_element_type=jnp.float32)
    summed = lax.psum(partial_value, "tensor")
    gram = (summed / COLS).astype(jnp.bfloat16)
    first = jnp.dot(gram, everyone, preferred_element_type=jnp.float32)
    first_half = first.astype(jnp.bfloat16)
    second = panel_product(gram, lax.all_gather(first_half, "fsdp", axis=0, tiled=True))
    updated = (
        coef_linear * moment.astype(jnp.float32)
        + coef_cubic * first_half.astype(jnp.float32)
        + coef_quintic * second
    )
    return updated.astype(jnp.bfloat16)


def solution(mesh):
    in_specs = (P("fsdp", "tensor"),)
    out_specs = P("fsdp", "tensor")
    return jax.shard_map(
        on_device, mesh=mesh, in_specs=in_specs, out_specs=out_specs, check_vma=False
    )
```

profile of v0, /device:TPU:1, one launch (start us, length us, event | category | flops | bytes accessed | tf_op | source)
XLA Modules:
  0.0 347.1 jit_solution(17450832696462256058)
XLA Ops:
  6.5 0.0 all-gather.3.cloned.1.call-start
  6.5 0.7 all-gather.3.cloned.1.call-update
  7.3 0.0 all-reduce.2.cloned.1.call-start
  7.3 89.9 %all-gather.3.cloned.1.call-done = bf16[4096,800]{0,1:T(8,128)(2,1)} async-done(((bf16[128,800]{0,1:T(8,128)(2,1)}), bf16[4096,800]{0,1:T(8,128)(2,1)}) %all-gather.3.cloned.1.call-update) | async-done | bytes 6553616 | tf_op jit(solution)/shard_map/all_gather | solution.py:20
  97.3 5.7 %fusion.4 = f32[128,4096]{1,0:T(8,128)} fusion(bf16[128,800]{0,1:T(8,128)(2,1)} %param.1, bf16[4096,800]{0,1:T(8,128)(2,1)} %all-gather.3.cloned.1.call-done), kind=kOutput, calls=%fused_computation.7 | convolution fusion | flops 838860800 | bytes 8855552 | tf_op jit(solution)/shard_map/dot_general | solution.py:21
  102.9 0.0 copy-start.1
  102.9 0.0 all-reduce.2.cloned.1.call-update
  102.9 0.0 all-gather.5.cloned.1.call-start
  103.0 137.0 %all-reduce.2.cloned.1.call-done = f32[128,4096]{1,0:T(8,128)} async-done(((f32[128,4096]{1,0:T(8,128)}), f32[128,4096]{1,0:T(8,128)}) %all-reduce.2.cloned.1.call-update) | async-done | bytes 2097168 | tf_op jit(solution)/shard_map/psum | solution.py:22
  240.0 0.0 copy-start
  240.0 6.2 %convolution_convert_fusion = bf16[128,800]{0,1:T(8,128)(2,1)} fusion(bf16[4096,800]{0,1:T(8,128)(2,1)} %all-gather.3.cloned.1.call-done, f32[128,4096]{1,0:T(8,128)} %all-reduce.2.cloned.1.call-done), kind=kOutput, calls=%fused_computation.4 | convolution fusion | flops 840011776 | bytes 8855552 | tf_op jit(solution)/shard_map/dot_general | solution.py:24
  246.1 0.0 all-gather.5.cloned.1.call-update
  246.2 89.0 %all-gather.5.cloned.1.call-done = bf16[4096,800]{0,1:T(8,128)(2,1)} async-done(((bf16[128,800]{0,1:T(8,128)(2,1)}), bf16[4096,800]{0,1:T(8,128)(2,1)}) %all-gather.5.cloned.1.call-update) | async-done | bytes 6553616 | tf_op jit(solution)/shard_map/all_gather | solution.py:26
  335.2 0.0 copy-done.1
  335.2 0.0 copy-done
  335.2 5.4 %fusion.1 = bf16[128,800]{0,1:T(8,128)(2,1)} fusion(bf16[4096,800]{0,1:T(8,128)(2,1)} %all-gather.5.cloned.1.call-done, bf16[128,800]{0,1:T(8,128)(2,1)} %convolution_convert_fusion, bf16[128,800]{0,1:T(8,128)(2,1)S(1)} %copy-done.1, f32[128,4096]{1,0:T(8,128)S(1)} %copy-done), kind=kOutput, calls=%fused_computation.3 | convolution fusion | flops 840728576 | bytes 9265152 | tf_op jit(solution)/shard_map/dot_general | solution.py:15
Async XLA Ops:
  6.5 90.7 %all-gather.3.cloned.1.call-start = ((), (), s32[]{:S(2)}) async-start(), calls=%async_computation | async-start | bytes 6758400 | tf_op jit(solution)/shard_map/all_gather | solution.py:20
  7.3 232.7 %all-reduce.2.cloned.1.call-start = ((), (), s32[]{:S(2)}) async-start(), calls=%async_computation.1 | async-start | bytes 4194304 | tf_op jit(solution)/shard_map/psum | solution.py:22
  102.9 232.3 %copy-start.1 = (bf16[128,800]{0,1:T(8,128)(2,1)S(1)}, bf16[128,800]{0,1:T(8,128)(2,1)}, u32[]{:S(2)}) copy-start(bf16[128,800]{0,1:T(8,128)(2,1)} %param.1) | copy-start | bytes 614404
  102.9 232.3 %all-gather.5.cloned.1.call-start = ((), (), s32[]{:S(2)}) async-start(), calls=%async_computation.2 | async-start | bytes 6758400 | tf_op jit(solution)/shard_map/all_gather | solution.py:26
  240.0 95.2 %copy-start = (f32[128,4096]{1,0:T(8,128)S(1)}, f32[128,4096]{1,0:T(8,128)}, u32[]{:S(2)}) copy-start(f32[128,4096]{1,0:T(8,128)} %all-reduce.2.cloned.1.call-done) | copy-start | bytes 6291460
Sparse Core Ops, SparseCore 0:
  10.4 86.7 all-gather.2
  103.1 136.8 all-reduce.1
  246.3 88.8 all-gather.4
where the time goes:
time: 347 us
  waiting for transfers between devices  317 us (91%)
  matrix products  17.2 us (5%)
  between operations  13.1 us (4%)
    psum x1, waiting for transfers between devices, on_device(): summed = lax.psum(partial_value, 'tensor')  137 us
    all_gather x1, waiting for transfers between devices, on_device(): everyone = lax.all_gather(moment, 'fsdp', axis=0, tiled=True)  89.9 us
    all_gather x1, waiting for transfers between devices, on_device(): lax.all_gather(first_half, 'fsdp', axis=0, tiled=True)  89 us
  transfers between devices with their start and end apart: 3, of which 3 were waited for; matrix products, arithmetic and copies ran while one was open for 0% of the time, Pallas kernels for 0%

commit v1 on v0

v1 whole, which is shorter than its diff:
```python
import jax
import jax.numpy as jnp
import numpy as np
from jax import lax
from jax.sharding import Mesh, PartitionSpec as P

COLS = 12800

coef_linear = 3.4445
coef_cubic = -4.775
coef_quintic = 2.0315

SPLIT = {"yh": 4, "x": 4, "core": 2, "yl": 2, "zh": 4, "zl": 2}
PAIRS = ("yl", "zl")
SUM_GROUP = PAIRS + ("zh",)
SWAP = [(0, 1), (1, 0)]


def spread(block, axes):
    return lax.all_to_all(jnp.broadcast_to(block[None], (4,) + block.shape), axes, 0, 0)


def collect(parts, own, axis):
    others = lax.all_to_all(parts, axis, 0, 0)
    index = lax.broadcasted_iota(jnp.int32, others.shape, 0)
    others = jnp.where(index == lax.axis_index(axis), 0.0, others.astype(jnp.float32))
    return own + jnp.sum(others, axis=0)


def both_cores(blocks):
    return jnp.stack([blocks, lax.ppermute(blocks, "core", SWAP)], axis=1)


def on_device(moment):
    mine = moment.T
    along, across = spread(mine, "x"), lax.all_gather(mine, "yh")
    along, across = lax.optimization_barrier((along, across))
    across = both_cores(across)

    gram = jnp.einsum("ecs,dfct->edsft", along, across, preferred_element_type=jnp.float32)
    gram = (gram / COLS).astype(jnp.bfloat16).reshape(16, *gram.shape[2:])
    gram = lax.all_to_all(gram, SUM_GROUP, 0, 0)
    gram = lax.reduce_precision(jnp.sum(gram.astype(jnp.float32), axis=0), 8, 7)
    gram = spread(lax.all_gather(gram.astype(jnp.bfloat16), "zh"), PAIRS)
    mine_only = lax.dynamic_slice_in_dim(gram, lax.axis_index("x"), 1, 0)

    def product(columns):
        def part(rows):
            return jnp.einsum("dfct,edsft->ecs", columns, rows, preferred_element_type=jnp.float32)

        return collect(part(gram).astype(jnp.bfloat16), part(mine_only)[0], "x")

    first = lax.reduce_precision(product(across), 8, 7)
    second = product(both_cores(lax.all_gather(first.astype(jnp.bfloat16), "yh")))

    updated = coef_linear * mine.astype(jnp.float32) + coef_cubic * first + coef_quintic * second
    return updated.astype(jnp.bfloat16).T


def solution(mesh):
    devices = np.asarray(mesh.devices).reshape(tuple(SPLIT.values()))
    fine = Mesh(devices, tuple(SPLIT))
    spec = P(("yh", "x", "core"), ("yl", "zh", "zl"))
    return jax.shard_map(on_device, mesh=fine, in_specs=(spec,), out_specs=spec, check_vma=False)
```

time: 347 us -> 160 us (0.46)
  waiting for transfers between devices: 317 us -> 12.4 us
  blocking collectives: 0 us -> 107 us
  starting transfers between devices: 0.08 us -> 27.8 us
  between operations: 13.1 us -> 0.09 us
  matrix products: 17.2 us -> 6.18 us
  local copies, waits for them, and re-layouts: 0.01 us -> 4.64 us
    all_gather x2 -> x0, waiting for transfers between devices: 179 us -> none  [the longest x1 89.9 us: on_device(): everyone = lax.all_gather(moment, 'fsdp', axis=0, tiled=True)]
    psum x1 -> x0, waiting for transfers between devices: 137 us -> none  [on_device(): summed = lax.psum(partial_value, 'tensor')]
    all_to_all x0 -> x3, blocking collectives: none -> 61.2 us  [the longest x1 35 us: on_device(): gram = lax.all_to_all(gram, SUM_GROUP, 0, 0)]
    all_gather x0 -> x3, blocking collectives: none -> 46.2 us  [the longest x1 19.5 us: on_device(): along, across = (spread(mine, 'x'), lax.all_gather(mine, 'yh'))]
    ppermute x0 -> x2, starting transfers between devices: none -> 18.6 us  [both_cores(): return jnp.stack([blocks, lax.ppermute(blocks, 'core', SWAP)], axis=1)]
    dot_general x3 -> x5, matrix products: 17.2 us -> 6.18 us  [the longest x4 4.9 us: part(): jnp.einsum('dfct,edsft->ecs', columns, rows, preferred_element_type=jnp.f...]
    all_to_all x0 -> x2, starting transfers between devices: none -> 9.19 us  [the longest x1 4.97 us: spread(): lax.all_to_all(jnp.broadcast_to(block[None], (4,) + block.shape), axes, 0...]
    all_to_all x0 -> x2, waiting for transfers between devices: none -> 8.51 us  [the longest x1 8.51 us: collect(): others = lax.all_to_all(parts, axis, 0, 0)]
  transfers between devices with their start and end apart: 3 -> 4, of which waited for: 3 -> 3; matrix products, arithmetic and copies ran while one was open for 0% -> 0% of each run, Pallas kernels for 0% -> 0%
where the time goes in v1:
time: 160 us; the launch traced here: 159 us
  blocking collectives  107 us (67%)
  starting transfers between devices  27.8 us (17%)
  waiting for transfers between devices  12.4 us (8%)
  matrix products  6.18 us (4%)
  local copies, waits for them, and re-layouts  4.64 us (3%)
    all_to_all x1, blocking collectives, on_device(): gram = lax.all_to_all(gram, SUM_GROUP, 0, 0)  35 us
    all_gather x1, blocking collectives, on_device(): along, across = (spread(mine, 'x'), lax.all_gather(mine, 'yh'))  19.5 us
    ppermute x2, starting transfers between devices, both_cores(): return jnp.stack([blocks, lax.ppermute(blocks, 'core', SWAP)], axis=1)  18.6 us
    all_to_all x1, blocking collectives, collect(): others = lax.all_to_all(parts, axis, 0, 0)  14.6 us
    all_gather x1, blocking collectives, on_device(): lax.all_gather(first.astype(jnp.bfloat16), 'yh')  14.6 us
    all_gather x1, blocking collectives, on_device(): gram = spread(lax.all_gather(gram.astype(jnp.bfloat16), 'zh'), PAIRS)  12.1 us
    all_to_all x1, blocking collectives, spread(): lax.all_to_all(jnp.broadcast_to(block[None], (4,) + block.shape), axes, 0...  11.5 us
    all_to_all x1, waiting for transfers between devices, collect(): others = lax.all_to_all(parts, axis, 0, 0)  8.51 us
  transfers between devices with their start and end apart: 4, of which 3 were waited for; matrix products, arithmetic and copies ran while one was open for 0% of the time, Pallas kernels for 0%

profile of v1, /device:TPU:1, one launch (start us, length us, event | category | flops | bytes accessed | tf_op | source)
XLA Modules:
  0.0 159.0 jit_solution(7648606693729526322)
XLA Ops:
  0.0 1.9 %broadcast_in_dim.19 = bf16[4,800,128]{2,1,0:T(8,128)(2,1)} broadcast(bf16[800,128]{1,0:T(8,128)(2,1)} %bitcast.132), dimensions={1,2} | broadcast | bytes 1024000 | tf_op jit(solution)/shard_map/broadcast_in_dim | solution.py:20
  1.9 5.0 %all-to-all-start = ((bf16[4,800,128]{2,1,0:T(8,128)(2,1)}), bf16[4,800,128]{2,1,0:T(8,128)(2,1)S(1)}, u32[]{:S(2)}, u32[]{:S(2)}) async-start(bf16[4,800,128]{2,1,0:T(8,128)(2,1)} %broadcast_in_dim.19), calls=%async_computation | async-start | bytes 1638400 | tf_op jit(solution)/shard_map/all_to_all | solution.py:20
  6.9 19.5 %all-gather = bf16[3200,128]{1,0:T(8,128)(2,1)S(1)} all-gather(bf16[800,128]{1,0:T(8,128)(2,1)S(1)} %bitcast.133), channel_id=2, replica_groups=mesh['yh'=4,'x'=4,'core'=2,'yl'=2,'zh'=4,'zl'=2] {'yh'}, dimensions={0}, use_global_device_ids=true | all-gather | bytes 1024000 | tf_op jit(solution)/shard_map/all_gather | solution.py:36
  26.4 6.9 %collective-permute-start = (bf16[4,800,128]{2,1,0:T(8,128)(2,1)S(1)}, bf16[4,800,128]{2,1,0:T(8,128)(2,1)S(1)}, u32[]{:S(2)}, u32[]{:S(2)}) collective-permute-start(bf16[4,800,128]{2,1,0:T(8,128)(2,1)S(1)} %bitcast.126), channel_id=1, source_target_pairs={{0,16},{16,0},{1,17},{17,1},{2,18},{18,2},{3,19},{19,3},{4,20},{20... | collective-permute-start | bytes 2457608 | tf_op jit(solution)/shard_map/ppermute | solution.py:31
  33.3 1.9 %collective-permute-done = bf16[4,800,128]{2,1,0:T(8,128)(2,1)S(1)} collective-permute-done((bf16[4,800,128]{2,1,0:T(8,128)(2,1)S(1)}, bf16[4,800,128]{2,1,0:T(8,128)(2,1)S(1)}, u32[]{:S(2)}, u32[]{:S(2)}) %collective-permute-start) | collective-permute-done | bytes 819232 | tf_op jit(solution)/shard_map/ppermute | solution.py:31
  35.3 0.9 copy-done.1
  36.2 1.3 fusion.12
  37.4 0.7 copy.14
  38.1 35.0 %all_to_all.25 = bf16[16,128,2,128]{3,1,2,0:T(8,128)(2,1)S(1)} all-to-all(bf16[16,128,2,128]{3,1,2,0:T(8,128)(2,1)S(1)} %bitcast.124), channel_id=1, replica_groups=mesh['yh'=4,'x'=4,'core'=2,'yl'=2,'zh'=4,'zl'=2] {'yl','zl','zh'}, dimensions={0} | all-to-all | bytes 2097152 | tf_op jit(solution)/shard_map/all_to_all | solution.py:42
  73.3 12.1 %all-gather.1 = bf16[512,2,128]{2,0,1:T(8,128)(2,1)S(1)} all-gather(bf16[128,2,128]{2,0,1:T(8,128)(2,1)S(1)} %reduce-precision_convert_fusion), channel_id=3, replica_groups=mesh['yh'=4,'x'=4,'core'=2,'yl'=2,'zh'=4,'zl'=2] {'zh'}, dimensions={0}, use_global_device_ids=true | all-gather | bytes 327680 | tf_op jit(solution)/shard_map/all_gather | solution.py:44
  85.7 11.5 %all_to_all.26 = bf16[4,4,128,2,128]{4,2,3,1,0:T(8,128)(2,1)S(1)} all-to-all(bf16[4,4,128,2,128]{4,2,3,1,0:T(8,128)(2,1)S(1)} %broadcast_in_dim.21), channel_id=1, replica_groups=mesh['yh'=4,'x'=4,'core'=2,'yl'=2,'zh'=4,'zl'=2] {'yl','zl'}, dimensions={0} | all-to-all | bytes 2097152 | tf_op jit(solution)/shard_map/all_to_all | solution.py:20
  97.2 2.0 %fusion.15 = bf16[4,800,128]{2,1,0:T(8,128)(2,1)} fusion(bf16[4,4,128,2,128]{4,2,3,1,0:T(8,128)(2,1)S(1)} %all_to_all.26, bf16[4,1,800,128]{3,2,1,0:T(8,128)(2,1)S(1)} %bitcast.135, bf16[4,1,800,128]{3,2,1,0:T(8,128)(2,1)S(1)} %bitcast.128), kind=kOutput, calls=%fused_computation.15 | convolution fusion | flops 840089600 | bytes 3506176 | tf_op jit(solution)/shard_map/dfct,edsft->ecs/dot_general | solution.py:49
  99.1 4.2 %all-to-all-start.3 = ((bf16[4,800,128]{2,1,0:T(8,128)(2,1)}), bf16[4,800,128]{2,1,0:T(8,128)(2,1)S(1)}, u32[]{:S(2)}, u32[]{:S(2)}) async-start(bf16[4,800,128]{2,1,0:T(8,128)(2,1)} %fusion.15), calls=%async_computation.3 | async-start | bytes 1638400 | tf_op jit(solution)/shard_map/all_to_all | solution.py:24
  103.3 8.5 %all-to-all-done.3 = bf16[4,800,128]{2,1,0:T(8,128)(2,1)S(1)} async-done(((bf16[4,800,128]{2,1,0:T(8,128)(2,1)}), bf16[4,800,128]{2,1,0:T(8,128)(2,1)S(1)}, u32[]{:S(2)}, u32[]{:S(2)}) %all-to-all-start.3) | async-done | bytes 819232 | tf_op jit(solution)/shard_map/all_to_all | solution.py:24
  111.9 0.3 select_reduce_fusion.1
  112.1 0.9 copy-done.3
  113.0 0.6 fusion.32
  113.6 14.6 %all_gather.14 = bf16[4,800,128]{2,1,0:T(8,128)(2,1)S(1)} all-gather(bf16[1,800,128]{2,1,0:T(8,128)(2,1)S(1)} %get-tuple-element.9), channel_id=1, replica_groups=mesh['yh'=4,'x'=4,'core'=2,'yl'=2,'zh'=4,'zl'=2] {'yh'}, dimensions={0}, use_global_device_ids=true | all-gather | bytes 1024000 | tf_op jit(solution)/shard_map/all_gather | solution.py:54
  128.2 11.7 %collective-permute-start.1 = (bf16[4,800,128]{2,1,0:T(8,128)(2,1)S(1)}, bf16[4,800,128]{2,1,0:T(8,128)(2,1)S(1)}, u32[]{:S(2)}, u32[]{:S(2)}) collective-permute-start(bf16[4,800,128]{2,1,0:T(8,128)(2,1)S(1)} %all_gather.14), channel_id=1, source_target_pairs={{0,16},{16,0},{1,17},{17,1},{2,18},{18,2},{3,19},{19,3},{4,20},{20... | collective-permute-start | bytes 2457608 | tf_op jit(solution)/shard_map/ppermute | solution.py:31
  139.9 1.9 %collective-permute-done.1 = bf16[4,800,128]{2,1,0:T(8,128)(2,1)S(1)} collective-permute-done((bf16[4,800,128]{2,1,0:T(8,128)(2,1)S(1)}, bf16[4,800,128]{2,1,0:T(8,128)(2,1)S(1)}, u32[]{:S(2)}, u32[]{:S(2)}) %collective-permute-start.1) | collective-permute-done | bytes 819232 | tf_op jit(solution)/shard_map/ppermute | solution.py:31
  141.8 1.0 fusion.18
  142.9 14.6 %all_to_all.27 = bf16[4,800,128]{2,1,0:T(8,128)(2,1)S(1)} all-to-all(bf16[4,800,128]{2,1,0:T(8,128)(2,1)S(1)} %fusion.18), channel_id=1, replica_groups=mesh['yh'=4,'x'=4,'core'=2,'yl'=2,'zh'=4,'zl'=2] {'x'}, dimensions={0} | all-to-all | bytes 1638400 | tf_op jit(solution)/shard_map/all_to_all | solution.py:24
  157.5 0.3 select_reduce_fusion
  157.7 1.3 fusion.25
  (12 shorter events, 0.4 us)
Async XLA Ops:
  1.9 5.0 %copy-start = (bf16[128,800]{0,1:T(8,128)(2,1)S(1)}, bf16[128,800]{0,1:T(8,128)(2,1)}, u32[]{:S(2)}) copy-start(bf16[128,800]{0,1:T(8,128)(2,1)} %param.1) | copy-start | bytes 614404
  1.9 24.5 %all-to-all-start = ((bf16[4,800,128]{2,1,0:T(8,128)(2,1)}), bf16[4,800,128]{2,1,0:T(8,128)(2,1)S(1)}, u32[]{:S(2)}, u32[]{:S(2)}) async-start(bf16[4,800,128]{2,1,0:T(8,128)(2,1)} %broadcast_in_dim.19), calls=%async_computation | async-start | bytes 1638400 | tf_op jit(solution)/shard_map/all_to_all | solution.py:20
  26.4 8.8 %collective-permute-start = (bf16[4,800,128]{2,1,0:T(8,128)(2,1)S(1)}, bf16[4,800,128]{2,1,0:T(8,128)(2,1)S(1)}, u32[]{:S(2)}, u32[]{:S(2)}) collective-permute-start(bf16[4,800,128]{2,1,0:T(8,128)(2,1)S(1)} %bitcast.126), channel_id=1, source_target_pairs={{0,16},{16,0},{1,17},{17,1},{2,18},{18,2},{3,19},{19,3},{4,20},{20... | collective-permute-start | bytes 2457608 | tf_op jit(solution)/shard_map/ppermute | solution.py:31
  35.3 0.9 copy-start.1
  85.7 11.5 %copy-start.2 = (bf16[4,800,128]{2,1,0:T(8,128)(2,1)S(1)}, bf16[4,800,128]{2,1,0:T(8,128)(2,1)}, u32[]{:S(2)}) copy-start(bf16[4,800,128]{2,1,0:T(8,128)(2,1)} %copy-done.1) | copy-start | bytes 2457604
  99.1 12.7 %all-to-all-start.3 = ((bf16[4,800,128]{2,1,0:T(8,128)(2,1)}), bf16[4,800,128]{2,1,0:T(8,128)(2,1)S(1)}, u32[]{:S(2)}, u32[]{:S(2)}) async-start(bf16[4,800,128]{2,1,0:T(8,128)(2,1)} %fusion.15), calls=%async_computation.3 | async-start | bytes 1638400 | tf_op jit(solution)/shard_map/all_to_all | solution.py:24
  111.9 1.1 copy-start.3
  128.2 13.6 %collective-permute-start.1 = (bf16[4,800,128]{2,1,0:T(8,128)(2,1)S(1)}, bf16[4,800,128]{2,1,0:T(8,128)(2,1)S(1)}, u32[]{:S(2)}, u32[]{:S(2)}) collective-permute-start(bf16[4,800,128]{2,1,0:T(8,128)(2,1)S(1)} %all_gather.14), channel_id=1, source_target_pairs={{0,16},{16,0},{1,17},{17,1},{2,18},{18,2},{3,19},{19,3},{4,20},{20... | collective-permute-start | bytes 2457608 | tf_op jit(solution)/shard_map/ppermute | solution.py:31

commit v2 on v1

--- a/solution.py
+++ b/solution.py
@@ -12,7 +12,6 @@
 
 SPLIT = {"yh": 4, "x": 4, "core": 2, "yl": 2, "zh": 4, "zl": 2}
 PAIRS = ("yl", "zl")
-SUM_GROUP = PAIRS + ("zh",)
 SWAP = [(0, 1), (1, 0)]
 
 
@@ -27,6 +26,10 @@
     return own + jnp.sum(others, axis=0)
 
 
+def total(parts):
+    return lax.reduce_precision(jnp.sum(parts.astype(jnp.float32), axis=0), 8, 7).astype(jnp.bfloat16)
+
+
 def both_cores(blocks):
     return jnp.stack([blocks, lax.ppermute(blocks, "core", SWAP)], axis=1)
 
@@ -38,10 +41,9 @@
     across = both_cores(across)
 
     gram = jnp.einsum("ecs,dfct->edsft", along, across, preferred_element_type=jnp.float32)
-    gram = (gram / COLS).astype(jnp.bfloat16).reshape(16, *gram.shape[2:])
-    gram = lax.all_to_all(gram, SUM_GROUP, 0, 0)
-    gram = lax.reduce_precision(jnp.sum(gram.astype(jnp.float32), axis=0), 8, 7)
-    gram = spread(lax.all_gather(gram.astype(jnp.bfloat16), "zh"), PAIRS)
+    gram = lax.all_to_all((gram / COLS).astype(jnp.bfloat16), PAIRS, 0, 0)
+    gram = total(lax.all_to_all(total(gram), "zh", 0, 0))
+    gram = spread(spread(gram, "zh"), PAIRS)
     mine_only = lax.dynamic_slice_in_dim(gram, lax.axis_index("x"), 1, 0)
 
     def product(columns):

time: 160 us -> 157 us (0.981)
  blocking collectives: 107 us -> 105 us
    all_to_all x1 -> x2, blocking collectives: 11.5 us -> 24.1 us  [spread(): lax.all_to_all(jnp.broadcast_to(block[None], (4,) + block.shape), axes, 0...]
    all_gather x1 -> x0, blocking collectives: 12.1 us -> none  [on_device(): gram = spread(lax.all_gather(gram.astype(jnp.bfloat16), 'zh'), PAIRS)]
    all_to_all x1 -> x2, blocking collectives: 35 us -> 33.6 us  [the longest x1 17.7 us: on_device(): gram = total(lax.all_to_all(total(gram), 'zh', 0, 0))]
where the time goes in v2:
time: 157 us; the launch traced here: 155 us
  blocking collectives  105 us (67%)
  starting transfers between devices  27 us (17%)
  waiting for transfers between devices  12.4 us (8%)
  matrix products  6.18 us (4%)
  local copies, waits for them, and re-layouts  3.28 us (2%)
    all_to_all x2, blocking collectives, spread(): lax.all_to_all(jnp.broadcast_to(block[None], (4,) + block.shape), axes, 0...  24.1 us
    all_gather x1, blocking collectives, on_device(): along, across = (spread(mine, 'x'), lax.all_gather(mine, 'yh'))  19.5 us
    ppermute x2, starting transfers between devices, both_cores(): return jnp.stack([blocks, lax.ppermute(blocks, 'core', SWAP)], axis=1)  18 us
    all_to_all x1, blocking collectives, on_device(): gram = total(lax.all_to_all(total(gram), 'zh', 0, 0))  17.7 us
    all_to_all x1, blocking collectives, on_device(): gram = lax.all_to_all((gram / COLS).astype(jnp.bfloat16), PAIRS, 0, 0)  15.9 us
    all_to_all x1, blocking collectives, collect(): others = lax.all_to_all(parts, axis, 0, 0)  14.6 us
    all_gather x1, blocking collectives, on_device(): lax.all_gather(first.astype(jnp.bfloat16), 'yh')  13.4 us
    all_to_all x1, waiting for transfers between devices, collect(): others = lax.all_to_all(parts, axis, 0, 0)  8.51 us
  transfers between devices with their start and end apart: 4, of which 3 were waited for; matrix products, arithmetic and copies ran while one was open for 0% of the time, Pallas kernels for 0%

profile of v2, /device:TPU:1, one launch (start us, length us, event | category | flops | bytes accessed | tf_op | source)
XLA Modules:
  0.0 155.0 jit_solution(2785032101937559111)
XLA Ops:
  0.0 1.9 %broadcast_in_dim.12 = bf16[4,800,128]{2,1,0:T(8,128)(2,1)} broadcast(bf16[800,128]{1,0:T(8,128)(2,1)} %bitcast.128), dimensions={1,2} | broadcast | bytes 1024000 | tf_op jit(solution)/shard_map/broadcast_in_dim | solution.py:19
  1.9 5.0 %all-to-all-start = ((bf16[4,800,128]{2,1,0:T(8,128)(2,1)}), bf16[4,800,128]{2,1,0:T(8,128)(2,1)S(1)}, u32[]{:S(2)}, u32[]{:S(2)}) async-start(bf16[4,800,128]{2,1,0:T(8,128)(2,1)} %broadcast_in_dim.12), calls=%async_computation | async-start | bytes 1638400 | tf_op jit(solution)/shard_map/all_to_all | solution.py:19
  6.9 19.5 %all-gather = bf16[3200,128]{1,0:T(8,128)(2,1)S(1)} all-gather(bf16[800,128]{1,0:T(8,128)(2,1)S(1)} %bitcast.129), channel_id=2, replica_groups=mesh['yh'=4,'x'=4,'core'=2,'yl'=2,'zh'=4,'zl'=2] {'yh'}, dimensions={0}, use_global_device_ids=true | all-gather | bytes 1024000 | tf_op jit(solution)/shard_map/all_gather | solution.py:39
  26.4 6.9 %collective-permute-start = (bf16[4,800,128]{2,1,0:T(8,128)(2,1)S(1)}, bf16[4,800,128]{2,1,0:T(8,128)(2,1)S(1)}, u32[]{:S(2)}, u32[]{:S(2)}) collective-permute-start(bf16[4,800,128]{2,1,0:T(8,128)(2,1)S(1)} %bitcast.122), channel_id=1, source_target_pairs={{0,16},{16,0},{1,17},{17,1},{2,18},{18,2},{3,19},{19,3},{4,20},{20... | collective-permute-start | bytes 2457608 | tf_op jit(solution)/shard_map/ppermute | solution.py:34
  33.3 1.9 %collective-permute-done = bf16[4,800,128]{2,1,0:T(8,128)(2,1)S(1)} collective-permute-done((bf16[4,800,128]{2,1,0:T(8,128)(2,1)S(1)}, bf16[4,800,128]{2,1,0:T(8,128)(2,1)S(1)}, u32[]{:S(2)}, u32[]{:S(2)}) %collective-permute-start) | collective-permute-done | bytes 819232 | tf_op jit(solution)/shard_map/ppermute | solution.py:34
  35.3 1.3 fusion.12
  36.6 15.9 %all_to_all.35 = bf16[4,4,128,2,128]{2,4,3,1,0:T(8,128)(2,1)S(1)} all-to-all(bf16[4,4,128,2,128]{2,4,3,1,0:T(8,128)(2,1)S(1)} %copy.13), channel_id=1, replica_groups=mesh['yh'=4,'x'=4,'core'=2,'yl'=2,'zh'=4,'zl'=2] {'yl','zl'}, dimensions={0} | all-to-all | bytes 2097152 | tf_op jit(solution)/shard_map/all_to_all | solution.py:44
  52.7 17.7 %all_to_all.36 = bf16[4,128,2,128]{1,3,2,0:T(8,128)(2,1)S(1)} all-to-all(bf16[4,128,2,128]{1,3,2,0:T(8,128)(2,1)S(1)} %reduce-precision_convert_fusion), channel_id=1, replica_groups=mesh['yh'=4,'x'=4,'core'=2,'yl'=2,'zh'=4,'zl'=2] {'zh'}, dimensions={0} | all-to-all | bytes 524288 | tf_op jit(solution)/shard_map/all_to_all | solution.py:45
  70.7 12.1 %all_to_all.37 = bf16[4,128,2,128]{3,1,2,0:T(8,128)(2,1)S(1)} all-to-all(bf16[4,128,2,128]{3,1,2,0:T(8,128)(2,1)S(1)} %broadcast_in_dim.27), channel_id=1, replica_groups=mesh['yh'=4,'x'=4,'core'=2,'yl'=2,'zh'=4,'zl'=2] {'zh'}, dimensions={0} | all-to-all | bytes 524288 | tf_op jit(solution)/shard_map/all_to_all | solution.py:19
  82.8 0.2 broadcast_in_dim.28
  83.0 12.0 %all_to_all.38 = bf16[4,4,128,2,128]{4,2,3,1,0:T(8,128)(2,1)S(1)} all-to-all(bf16[4,4,128,2,128]{4,2,3,1,0:T(8,128)(2,1)S(1)} %broadcast_in_dim.28), channel_id=1, replica_groups=mesh['yh'=4,'x'=4,'core'=2,'yl'=2,'zh'=4,'zl'=2] {'yl','zl'}, dimensions={0} | all-to-all | bytes 2097152 | tf_op jit(solution)/shard_map/all_to_all | solution.py:19
  95.1 2.0 %fusion.15 = bf16[4,800,128]{2,1,0:T(8,128)(2,1)} fusion(bf16[4,4,128,2,128]{4,2,3,1,0:T(8,128)(2,1)S(1)} %all_to_all.38, bf16[4,1,800,128]{3,2,1,0:T(8,128)(2,1)S(1)} %bitcast.131, bf16[4,1,800,128]{3,2,1,0:T(8,128)(2,1)S(1)} %bitcast.124), kind=kOutput, calls=%fused_computation.15 | convolution fusion | flops 840089600 | bytes 3506176 | tf_op jit(solution)/shard_map/dfct,edsft->ecs/dot_general | solution.py:51
  97.0 4.0 %all-to-all-start.5 = ((bf16[4,800,128]{2,1,0:T(8,128)(2,1)}), bf16[4,800,128]{2,1,0:T(8,128)(2,1)S(1)}, u32[]{:S(2)}, u32[]{:S(2)}) async-start(bf16[4,800,128]{2,1,0:T(8,128)(2,1)} %fusion.15), calls=%async_computation.5 | async-start | bytes 1638400 | tf_op jit(solution)/shard_map/all_to_all | solution.py:23
  101.0 8.5 %all-to-all-done.5 = bf16[4,800,128]{2,1,0:T(8,128)(2,1)S(1)} async-done(((bf16[4,800,128]{2,1,0:T(8,128)(2,1)}), bf16[4,800,128]{2,1,0:T(8,128)(2,1)S(1)}, u32[]{:S(2)}, u32[]{:S(2)}) %all-to-all-start.5) | async-done | bytes 819232 | tf_op jit(solution)/shard_map/all_to_all | solution.py:23
  109.5 0.3 select_reduce_fusion.1
  109.8 0.9 copy-done.3
  110.7 0.6 fusion.32
  111.3 13.4 %all_gather.9 = bf16[4,800,128]{2,1,0:T(8,128)(2,1)S(1)} all-gather(bf16[1,800,128]{2,1,0:T(8,128)(2,1)S(1)} %get-tuple-element.9), channel_id=1, replica_groups=mesh['yh'=4,'x'=4,'core'=2,'yl'=2,'zh'=4,'zl'=2] {'yh'}, dimensions={0}, use_global_device_ids=true | all-gather | bytes 1024000 | tf_op jit(solution)/shard_map/all_gather | solution.py:56
  124.7 11.1 %collective-permute-start.1 = (bf16[4,800,128]{2,1,0:T(8,128)(2,1)S(1)}, bf16[4,800,128]{2,1,0:T(8,128)(2,1)S(1)}, u32[]{:S(2)}, u32[]{:S(2)}) collective-permute-start(bf16[4,800,128]{2,1,0:T(8,128)(2,1)S(1)} %all_gather.9), channel_id=1, source_target_pairs={{0,16},{16,0},{1,17},{17,1},{2,18},{18,2},{3,19},{19,3},{4,20},{20... | collective-permute-start | bytes 2457608 | tf_op jit(solution)/shard_map/ppermute | solution.py:34
  135.8 1.9 %collective-permute-done.1 = bf16[4,800,128]{2,1,0:T(8,128)(2,1)S(1)} collective-permute-done((bf16[4,800,128]{2,1,0:T(8,128)(2,1)S(1)}, bf16[4,800,128]{2,1,0:T(8,128)(2,1)S(1)}, u32[]{:S(2)}, u32[]{:S(2)}) %collective-permute-start.1) | collective-permute-done | bytes 819232 | tf_op jit(solution)/shard_map/ppermute | solution.py:34
  137.7 1.0 fusion.18
  138.8 14.6 %all_to_all.39 = bf16[4,800,128]{2,1,0:T(8,128)(2,1)S(1)} all-to-all(bf16[4,800,128]{2,1,0:T(8,128)(2,1)S(1)} %fusion.18), channel_id=1, replica_groups=mesh['yh'=4,'x'=4,'core'=2,'yl'=2,'zh'=4,'zl'=2] {'x'}, dimensions={0} | all-to-all | bytes 1638400 | tf_op jit(solution)/shard_map/all_to_all | solution.py:23
  153.4 0.3 select_reduce_fusion
  153.7 1.3 fusion.25
  (16 shorter events, 0.5 us)
Async XLA Ops:
  1.9 5.0 %copy-start = (bf16[128,800]{0,1:T(8,128)(2,1)S(1)}, bf16[128,800]{0,1:T(8,128)(2,1)}, u32[]{:S(2)}) copy-start(bf16[128,800]{0,1:T(8,128)(2,1)} %param.1) | copy-start | bytes 614404
  1.9 24.5 %all-to-all-start = ((bf16[4,800,128]{2,1,0:T(8,128)(2,1)}), bf16[4,800,128]{2,1,0:T(8,128)(2,1)S(1)}, u32[]{:S(2)}, u32[]{:S(2)}) async-start(bf16[4,800,128]{2,1,0:T(8,128)(2,1)} %broadcast_in_dim.12), calls=%async_computation | async-start | bytes 1638400 | tf_op jit(solution)/shard_map/all_to_all | solution.py:19
  26.4 8.8 %collective-permute-start = (bf16[4,800,128]{2,1,0:T(8,128)(2,1)S(1)}, bf16[4,800,128]{2,1,0:T(8,128)(2,1)S(1)}, u32[]{:S(2)}, u32[]{:S(2)}) collective-permute-start(bf16[4,800,128]{2,1,0:T(8,128)(2,1)S(1)} %bitcast.122), channel_id=1, source_target_pairs={{0,16},{16,0},{1,17},{17,1},{2,18},{18,2},{3,19},{19,3},{4,20},{20... | collective-permute-start | bytes 2457608 | tf_op jit(solution)/shard_map/ppermute | solution.py:34
  35.3 1.3 copy-start.1
  83.0 12.0 %copy-start.2 = (bf16[4,800,128]{2,1,0:T(8,128)(2,1)S(1)}, bf16[4,800,128]{2,1,0:T(8,128)(2,1)}, u32[]{:S(2)}) copy-start(bf16[4,800,128]{2,1,0:T(8,128)(2,1)} %copy-done.1) | copy-start | bytes 2457604
  97.0 12.5 %all-to-all-start.5 = ((bf16[4,800,128]{2,1,0:T(8,128)(2,1)}), bf16[4,800,128]{2,1,0:T(8,128)(2,1)S(1)}, u32[]{:S(2)}, u32[]{:S(2)}) async-start(bf16[4,800,128]{2,1,0:T(8,128)(2,1)} %fusion.15), calls=%async_computation.5 | async-start | bytes 1638400 | tf_op jit(solution)/shard_map/all_to_all | solution.py:23
  109.5 1.1 copy-start.3
  124.7 13.1 %collective-permute-start.1 = (bf16[4,800,128]{2,1,0:T(8,128)(2,1)S(1)}, bf16[4,800,128]{2,1,0:T(8,128)(2,1)S(1)}, u32[]{:S(2)}, u32[]{:S(2)}) collective-permute-start(bf16[4,800,128]{2,1,0:T(8,128)(2,1)S(1)} %all_gather.9), channel_id=1, source_target_pairs={{0,16},{16,0},{1,17},{17,1},{2,18},{18,2},{3,19},{19,3},{4,20},{20... | collective-permute-start | bytes 2457608 | tf_op jit(solution)/shard_map/ppermute | solution.py:34

commit v3 on v2

--- a/solution.py
+++ b/solution.py
@@ -19,11 +19,11 @@
     return lax.all_to_all(jnp.broadcast_to(block[None], (4,) + block.shape), axes, 0, 0)
 
 
-def collect(parts, own, axis):
-    others = lax.all_to_all(parts, axis, 0, 0)
-    index = lax.broadcasted_iota(jnp.int32, others.shape, 0)
-    others = jnp.where(index == lax.axis_index(axis), 0.0, others.astype(jnp.float32))
-    return own + jnp.sum(others, axis=0)
+def others(parts, axis):
+    parts = lax.all_to_all(parts, axis, 0, 0)
+    index = lax.broadcasted_iota(jnp.int32, parts.shape, 0)
+    parts = jnp.where(index == lax.axis_index(axis), 0.0, parts.astype(jnp.float32))
+    return jnp.sum(parts, axis=0)
 
 
 def total(parts):
@@ -50,12 +50,15 @@
         def part(rows):
             return jnp.einsum("dfct,edsft->ecs", columns, rows, preferred_element_type=jnp.float32)
 
-        return collect(part(gram).astype(jnp.bfloat16), part(mine_only)[0], "x")
+        return part(gram).astype(jnp.bfloat16), part(mine_only)[0]
 
-    first = lax.reduce_precision(product(across), 8, 7)
-    second = product(both_cores(lax.all_gather(first.astype(jnp.bfloat16), "yh")))
-
-    updated = coef_linear * mine.astype(jnp.float32) + coef_cubic * first + coef_quintic * second
+    parts, own = product(across)
+    own = lax.optimization_barrier(own)
+    first = lax.reduce_precision(own + others(parts, "x"), 8, 7)
+    parts, own = product(both_cores(lax.all_gather(first.astype(jnp.bfloat16), "yh")))
+    known = coef_linear * mine.astype(jnp.float32) + coef_cubic * first + coef_quintic * own
+    known = lax.optimization_barrier(known)
+    updated = known + coef_quintic * others(parts, "x")
     return updated.astype(jnp.bfloat16).T
 
 

time: 157 us -> 159 us (1.013)
  blocking collectives: 105 us -> 90.8 us
  waiting for transfers between devices: 12.4 us -> 19.7 us
  matrix products: 6.18 us -> 11.5 us
  starting transfers between devices: 27 us -> 30.5 us
    all_to_all x1 -> x0, blocking collectives: 14.6 us -> none  [collect(): others = lax.all_to_all(parts, axis, 0, 0)]
    all_to_all x1 -> x2, waiting for transfers between devices: 8.51 us -> 15.7 us  [others(): parts = lax.all_to_all(parts, axis, 0, 0)]
    dot_general x4, matrix products: 4.9 us -> 10.2 us  [part(): jnp.einsum('dfct,edsft->ecs', columns, rows, preferred_element_type=jnp.f...]
    all_to_all x1 -> x2, starting transfers between devices: 3.98 us -> 7.47 us  [others(): parts = lax.all_to_all(parts, axis, 0, 0)]
  transfers between devices with their start and end apart: 4 -> 5, of which waited for: 3 -> 4; matrix products, arithmetic and copies ran while one was open for 0% -> 3% of each run, Pallas kernels for 0% -> 0%
where the time goes in v3:
time: 159 us; the launch traced here: 157 us
  blocking collectives  90.8 us (57%)
  starting transfers between devices  30.5 us (19%)
  waiting for transfers between devices  19.7 us (12%)
  matrix products  11.5 us (7%)
  local copies, waits for them, and re-layouts  2.4 us (2%)
    all_to_all x2, blocking collectives, spread(): lax.all_to_all(jnp.broadcast_to(block[None], (4,) + block.shape), axes, 0...  24.1 us
    all_gather x1, blocking collectives, on_device(): along, across = (spread(mine, 'x'), lax.all_gather(mine, 'yh'))  19.5 us
    ppermute x2, starting transfers between devices, both_cores(): return jnp.stack([blocks, lax.ppermute(blocks, 'core', SWAP)], axis=1)  18.1 us
    all_to_all x1, blocking collectives, on_device(): gram = total(lax.all_to_all(total(gram), 'zh', 0, 0))  17.7 us
    all_to_all x1, blocking collectives, on_device(): gram = lax.all_to_all((gram / COLS).astype(jnp.bfloat16), PAIRS, 0, 0)  15.9 us
    all_to_all x2, waiting for transfers between devices, others(): parts = lax.all_to_all(parts, axis, 0, 0)  15.7 us
    all_gather x1, blocking collectives, on_device(): lax.all_gather(first.astype(jnp.bfloat16), 'yh')  13.6 us
    dot_general x4, matrix products, part(): jnp.einsum('dfct,edsft->ecs', columns, rows, preferred_element_type=jnp.f...  10.2 us
  transfers between devices with their start and end apart: 5, of which 4 were waited for; matrix products, arithmetic and copies ran while one was open for 3% of the time, Pallas kernels for 0%

profile of v3, /device:TPU:1, one launch (start us, length us, event | category | flops | bytes accessed | tf_op | source)
XLA Modules:
  0.0 156.6 jit_solution(9331128392754157800)
XLA Ops:
  0.0 1.9 %broadcast_in_dim.12 = bf16[4,800,128]{2,1,0:T(8,128)(2,1)} broadcast(bf16[800,128]{1,0:T(8,128)(2,1)} %bitcast.113), dimensions={1,2} | broadcast | bytes 1024000 | tf_op jit(solution)/shard_map/broadcast_in_dim | solution.py:19
  1.9 5.0 %all-to-all-start = ((bf16[4,800,128]{2,1,0:T(8,128)(2,1)}), bf16[4,800,128]{2,1,0:T(8,128)(2,1)S(1)}, u32[]{:S(2)}, u32[]{:S(2)}) async-start(bf16[4,800,128]{2,1,0:T(8,128)(2,1)} %broadcast_in_dim.12), calls=%async_computation | async-start | bytes 1638400 | tf_op jit(solution)/shard_map/all_to_all | solution.py:19
  6.9 19.5 %all-gather = bf16[3200,128]{1,0:T(8,128)(2,1)S(1)} all-gather(bf16[800,128]{1,0:T(8,128)(2,1)S(1)} %bitcast.114), channel_id=2, replica_groups=mesh['yh'=4,'x'=4,'core'=2,'yl'=2,'zh'=4,'zl'=2] {'yh'}, dimensions={0}, use_global_device_ids=true | all-gather | bytes 1024000 | tf_op jit(solution)/shard_map/all_gather | solution.py:39
  26.4 6.9 %collective-permute-start = (bf16[4,800,128]{2,1,0:T(8,128)(2,1)S(1)}, bf16[4,800,128]{2,1,0:T(8,128)(2,1)S(1)}, u32[]{:S(2)}, u32[]{:S(2)}) collective-permute-start(bf16[4,800,128]{2,1,0:T(8,128)(2,1)S(1)} %bitcast.106), channel_id=1, source_target_pairs={{0,16},{16,0},{1,17},{17,1},{2,18},{18,2},{3,19},{19,3},{4,20},{20... | collective-permute-start | bytes 2457608 | tf_op jit(solution)/shard_map/ppermute | solution.py:34
  33.3 1.9 %collective-permute-done = bf16[4,800,128]{2,1,0:T(8,128)(2,1)S(1)} collective-permute-done((bf16[4,800,128]{2,1,0:T(8,128)(2,1)S(1)}, bf16[4,800,128]{2,1,0:T(8,128)(2,1)S(1)}, u32[]{:S(2)}, u32[]{:S(2)}) %collective-permute-start) | collective-permute-done | bytes 819232 | tf_op jit(solution)/shard_map/ppermute | solution.py:34
  35.3 1.3 fusion.12
  36.6 15.9 %all_to_all.35 = bf16[4,4,128,2,128]{2,4,3,1,0:T(8,128)(2,1)S(1)} all-to-all(bf16[4,4,128,2,128]{2,4,3,1,0:T(8,128)(2,1)S(1)} %copy.14), channel_id=1, replica_groups=mesh['yh'=4,'x'=4,'core'=2,'yl'=2,'zh'=4,'zl'=2] {'yl','zl'}, dimensions={0} | all-to-all | bytes 2097152 | tf_op jit(solution)/shard_map/all_to_all | solution.py:44
  52.7 17.7 %all_to_all.36 = bf16[4,128,2,128]{1,3,2,0:T(8,128)(2,1)S(1)} all-to-all(bf16[4,128,2,128]{1,3,2,0:T(8,128)(2,1)S(1)} %reduce-precision_convert_fusion), channel_id=1, replica_groups=mesh['yh'=4,'x'=4,'core'=2,'yl'=2,'zh'=4,'zl'=2] {'zh'}, dimensions={0} | all-to-all | bytes 524288 | tf_op jit(solution)/shard_map/all_to_all | solution.py:45
  70.7 12.1 %all_to_all.37 = bf16[4,128,2,128]{3,1,2,0:T(8,128)(2,1)S(1)} all-to-all(bf16[4,128,2,128]{3,1,2,0:T(8,128)(2,1)S(1)} %broadcast_in_dim.27), channel_id=1, replica_groups=mesh['yh'=4,'x'=4,'core'=2,'yl'=2,'zh'=4,'zl'=2] {'zh'}, dimensions={0} | all-to-all | bytes 524288 | tf_op jit(solution)/shard_map/all_to_all | solution.py:19
  83.1 12.0 %all_to_all.38 = bf16[4,4,128,2,128]{4,2,3,1,0:T(8,128)(2,1)S(1)} all-to-all(bf16[4,4,128,2,128]{4,2,3,1,0:T(8,128)(2,1)S(1)} %broadcast_in_dim.28), channel_id=1, replica_groups=mesh['yh'=4,'x'=4,'core'=2,'yl'=2,'zh'=4,'zl'=2] {'yl','zl'}, dimensions={0} | all-to-all | bytes 2097152 | tf_op jit(solution)/shard_map/all_to_all | solution.py:19
  95.1 2.0 %fusion.15 = bf16[4,800,128]{2,1,0:T(8,128)(2,1)} fusion(bf16[4,4,128,2,128]{4,2,3,1,0:T(8,128)(2,1)S(1)} %all_to_all.38, bf16[4,1,800,128]{3,2,1,0:T(8,128)(2,1)S(1)} %bitcast.117, bf16[4,1,800,128]{3,2,1,0:T(8,128)(2,1)S(1)} %bitcast.108), kind=kOutput, calls=%fused_computation.15 | convolution fusion | flops 840089600 | bytes 3506176 | tf_op jit(solution)/shard_map/dfct,edsft->ecs/dot_general | solution.py:51
  97.0 4.0 %all-to-all-start.5 = ((bf16[4,800,128]{2,1,0:T(8,128)(2,1)}), bf16[4,800,128]{2,1,0:T(8,128)(2,1)S(1)}, u32[]{:S(2)}, u32[]{:S(2)}) async-start(bf16[4,800,128]{2,1,0:T(8,128)(2,1)} %fusion.15), calls=%async_computation.5 | async-start | bytes 1638400 | tf_op jit(solution)/shard_map/all_to_all | solution.py:23
  101.0 2.5 %convolution_bitcast_fusion.1 = f32[800,128]{1,0:T(8,128)} fusion(bf16[4,1,800,128]{3,2,1,0:T(8,128)(2,1)} %bitcast.116, bf16[4,1,800,128]{3,2,1,0:T(8,128)(2,1)S(1)} %bitcast.109, bf16[4,4,128,2,128]{4,2,3,1,0:T(8,128)(2,1)S(1)} %all_to_all.38, s32[]{:T(128)S(6)} %select_n.10), kind=kOutput, calls=%fused_computation.18 | convolution fusion | flops 210534400 | bytes 2310148 | tf_op jit(solution)/shard_map/dfct,edsft->ecs/dot_general | solution.py:51
  103.5 6.0 %all-to-all-done.5 = bf16[4,800,128]{2,1,0:T(8,128)(2,1)S(1)} async-done(((bf16[4,800,128]{2,1,0:T(8,128)(2,1)}), bf16[4,800,128]{2,1,0:T(8,128)(2,1)S(1)}, u32[]{:S(2)}, u32[]{:S(2)}) %all-to-all-start.5) | async-done | bytes 819232 | tf_op jit(solution)/shard_map/all_to_all | solution.py:23
  109.5 0.3 select_reduce_fusion.1
  109.8 13.6 %all-gather.1 = bf16[3200,128]{1,0:T(8,128)(2,1)S(1)} all-gather(bf16[800,128]{1,0:T(8,128)(2,1)S(1)} %fusion.30), channel_id=3, replica_groups=mesh['yh'=4,'x'=4,'core'=2,'yl'=2,'zh'=4,'zl'=2] {'yh'}, dimensions={0}, use_global_device_ids=true | all-gather | bytes 1024000 | tf_op jit(solution)/shard_map/all_gather | solution.py:58
  123.4 11.2 %collective-permute-start.1 = (bf16[4,800,128]{2,1,0:T(8,128)(2,1)S(1)}, bf16[4,800,128]{2,1,0:T(8,128)(2,1)}, u32[]{:S(2)}, u32[]{:S(2)}) collective-permute-start(bf16[4,800,128]{2,1,0:T(8,128)(2,1)S(1)} %bitcast.110), channel_id=1, source_target_pairs={{0,16},{16,0},{1,17},{17,1},{2,18},{18,2},{3,19},{19,3},{4,20},{20... | collective-permute-start | bytes 2457608 | tf_op jit(solution)/shard_map/ppermute | solution.py:34
  134.6 2.1 %collective-permute-done.1 = bf16[4,800,128]{2,1,0:T(8,128)(2,1)} collective-permute-done((bf16[4,800,128]{2,1,0:T(8,128)(2,1)S(1)}, bf16[4,800,128]{2,1,0:T(8,128)(2,1)}, u32[]{:S(2)}, u32[]{:S(2)}) %collective-permute-start.1) | collective-permute-done | bytes 819232 | tf_op jit(solution)/shard_map/ppermute | solution.py:34
  136.7 3.1 %fusion.18 = bf16[4,800,128]{2,1,0:T(8,128)(2,1)} fusion(bf16[4,4,128,2,128]{4,2,3,1,0:T(8,128)(2,1)S(1)} %all_to_all.38, bf16[4,1,800,128]{3,2,1,0:T(8,128)(2,1)} %bitcast.23, bf16[4,1,800,128]{3,2,1,0:T(8,128)(2,1)S(1)} %bitcast.111), kind=kOutput, calls=%fused_computation.16 | convolution fusion | flops 840089600 | bytes 3506176 | tf_op jit(solution)/shard_map/dfct,edsft->ecs/dot_general | solution.py:51
  139.8 3.5 %all-to-all-start.6 = ((bf16[4,800,128]{2,1,0:T(8,128)(2,1)}), bf16[4,800,128]{2,1,0:T(8,128)(2,1)S(1)}, u32[]{:S(2)}, u32[]{:S(2)}) async-start(bf16[4,800,128]{2,1,0:T(8,128)(2,1)} %fusion.18), calls=%async_computation.6 | async-start | bytes 1638400 | tf_op jit(solution)/shard_map/all_to_all | solution.py:23
  143.3 2.6 %fusion.23 = f32[800,128]{1,0:T(8,128)} fusion(bf16[4,1,800,128]{3,2,1,0:T(8,128)(2,1)} %bitcast.23, bf16[4,1,800,128]{3,2,1,0:T(8,128)(2,1)S(1)} %bitcast.112, bf16[4,4,128,2,128]{4,2,3,1,0:T(8,128)(2,1)S(1)} %all_to_all.38, s32[]{:T(128)S(6)} %select_n.10, f32[800,128]{1,0:T(8,128)} %convolution_bitcast_fusion.1, f32[800,128]{1,0:T(8,128)S(1)} %select_reduce_fusion.1, ...), kind=kOutput, calls=%fused_computation.21 | convolution fusion | flops 211353600 | bytes 3334148 | tf_op jit(solution)/shard_map/dfct,edsft->ecs/dot_general | solution.py:51
  145.9 9.7 %all-to-all-done.6 = bf16[4,800,128]{2,1,0:T(8,128)(2,1)S(1)} async-done(((bf16[4,800,128]{2,1,0:T(8,128)(2,1)}), bf16[4,800,128]{2,1,0:T(8,128)(2,1)S(1)}, u32[]{:S(2)}, u32[]{:S(2)}) %all-to-all-start.6) | async-done | bytes 819232 | tf_op jit(solution)/shard_map/all_to_all | solution.py:23
  155.6 0.3 select_reduce_fusion
  155.9 0.7 fusion.29
  (21 shorter events, 0.8 us)
Async XLA Ops:
  1.9 5.0 %copy-start = (bf16[128,800]{0,1:T(8,128)(2,1)S(1)}, bf16[128,800]{0,1:T(8,128)(2,1)}, u32[]{:S(2)}) copy-start(bf16[128,800]{0,1:T(8,128)(2,1)} %param.1) | copy-start | bytes 614404
  1.9 24.5 %all-to-all-start = ((bf16[4,800,128]{2,1,0:T(8,128)(2,1)}), bf16[4,800,128]{2,1,0:T(8,128)(2,1)S(1)}, u32[]{:S(2)}, u32[]{:S(2)}) async-start(bf16[4,800,128]{2,1,0:T(8,128)(2,1)} %broadcast_in_dim.12), calls=%async_computation | async-start | bytes 1638400 | tf_op jit(solution)/shard_map/all_to_all | solution.py:19
  26.4 8.8 %collective-permute-start = (bf16[4,800,128]{2,1,0:T(8,128)(2,1)S(1)}, bf16[4,800,128]{2,1,0:T(8,128)(2,1)S(1)}, u32[]{:S(2)}, u32[]{:S(2)}) collective-permute-start(bf16[4,800,128]{2,1,0:T(8,128)(2,1)S(1)} %bitcast.106), channel_id=1, source_target_pairs={{0,16},{16,0},{1,17},{17,1},{2,18},{18,2},{3,19},{19,3},{4,20},{20... | collective-permute-start | bytes 2457608 | tf_op jit(solution)/shard_map/ppermute | solution.py:34
  35.3 1.4 copy-start.3
  83.0 12.0 %copy-start.4 = (bf16[4,800,128]{2,1,0:T(8,128)(2,1)S(1)}, bf16[4,800,128]{2,1,0:T(8,128)(2,1)}, u32[]{:S(2)}) copy-start(bf16[4,800,128]{2,1,0:T(8,128)(2,1)} %copy-done.3) | copy-start | bytes 2457604
  97.0 12.5 %all-to-all-start.5 = ((bf16[4,800,128]{2,1,0:T(8,128)(2,1)}), bf16[4,800,128]{2,1,0:T(8,128)(2,1)S(1)}, u32[]{:S(2)}, u32[]{:S(2)}) async-start(bf16[4,800,128]{2,1,0:T(8,128)(2,1)} %fusion.15), calls=%async_computation.5 | async-start | bytes 1638400 | tf_op jit(solution)/shard_map/all_to_all | solution.py:23
  103.5 6.3 %copy-start.1 = (f32[800,128]{1,0:T(8,128)S(1)}, f32[800,128]{1,0:T(8,128)}, u32[]{:S(2)}) copy-start(f32[800,128]{1,0:T(8,128)} %convolution_bitcast_fusion.1) | copy-start | bytes 1228804
  123.4 13.3 %collective-permute-start.1 = (bf16[4,800,128]{2,1,0:T(8,128)(2,1)S(1)}, bf16[4,800,128]{2,1,0:T(8,128)(2,1)}, u32[]{:S(2)}, u32[]{:S(2)}) collective-permute-start(bf16[4,800,128]{2,1,0:T(8,128)(2,1)S(1)} %bitcast.110), channel_id=1, source_target_pairs={{0,16},{16,0},{1,17},{17,1},{2,18},{18,2},{3,19},{19,3},{4,20},{20... | collective-permute-start | bytes 2457608 | tf_op jit(solution)/shard_map/ppermute | solution.py:34
  139.8 15.9 %all-to-all-start.6 = ((bf16[4,800,128]{2,1,0:T(8,128)(2,1)}), bf16[4,800,128]{2,1,0:T(8,128)(2,1)S(1)}, u32[]{:S(2)}, u32[]{:S(2)}) async-start(bf16[4,800,128]{2,1,0:T(8,128)(2,1)} %fusion.18), calls=%async_computation.6 | async-start | bytes 1638400 | tf_op jit(solution)/shard_map/all_to_all | solution.py:23
  145.9 10.0 %copy-start.2 = (f32[800,128]{1,0:T(8,128)S(1)}, f32[800,128]{1,0:T(8,128)}, u32[]{:S(2)}) copy-start(f32[800,128]{1,0:T(8,128)} %fusion.23) | copy-start | bytes 1228804

commit v4 on v3

--- a/solution.py
+++ b/solution.py
@@ -56,9 +56,9 @@
     own = lax.optimization_barrier(own)
     first = lax.reduce_precision(own + others(parts, "x"), 8, 7)
     parts, own = product(both_cores(lax.all_gather(first.astype(jnp.bfloat16), "yh")))
-    known = coef_linear * mine.astype(jnp.float32) + coef_cubic * first + coef_quintic * own
-    known = lax.optimization_barrier(known)
-    updated = known + coef_quintic * others(parts, "x")
+    second = own + others(parts, "x")
+
+    updated = coef_linear * mine.astype(jnp.float32) + coef_cubic * first + coef_quintic * second
     return updated.astype(jnp.bfloat16).T
 
 

time: 159 us -> 156 us (0.981)
  blocking collectives: 90.8 us -> 105 us
  waiting for transfers between devices: 19.7 us -> 10.6 us
  matrix products: 11.5 us -> 7.3 us
  starting transfers between devices: 30.5 us -> 27 us
    all_to_all x0 -> x1, blocking collectives: none -> 14.6 us  [others(): parts = lax.all_to_all(parts, axis, 0, 0)]
    all_to_all x2 -> x1, waiting for transfers between devices: 15.7 us -> 6.77 us  [others(): parts = lax.all_to_all(parts, axis, 0, 0)]
    dot_general x4, matrix products: 10.2 us -> 6.02 us  [part(): jnp.einsum('dfct,edsft->ecs', columns, rows, preferred_element_type=jnp.f...]
    all_to_all x2 -> x1, starting transfers between devices: 7.47 us -> 3.97 us  [others(): parts = lax.all_to_all(parts, axis, 0, 0)]
  transfers between devices with their start and end apart: 5 -> 4, of which waited for: 4 -> 3; matrix products, arithmetic and copies ran while one was open for 3% -> 1% of each run, Pallas kernels for 0% -> 0%
where the time goes in v4:
time: 156 us; the launch traced here: 154 us
  blocking collectives  105 us (67%)
  starting transfers between devices  27 us (17%)
  waiting for transfers between devices  10.6 us (7%)
  matrix products  7.3 us (5%)
  local copies, waits for them, and re-layouts  2.38 us (2%)
    all_to_all x2, blocking collectives, spread(): lax.all_to_all(jnp.broadcast_to(block[None], (4,) + block.shape), axes, 0...  24 us
    all_gather x1, blocking collectives, on_device(): along, across = (spread(mine, 'x'), lax.all_gather(mine, 'yh'))  19.5 us
    ppermute x2, starting transfers between devices, both_cores(): return jnp.stack([blocks, lax.ppermute(blocks, 'core', SWAP)], axis=1)  18.1 us
    all_to_all x1, blocking collectives, on_device(): gram = total(lax.all_to_all(total(gram), 'zh', 0, 0))  17.7 us
    all_to_all x1, blocking collectives, on_device(): gram = lax.all_to_all((gram / COLS).astype(jnp.bfloat16), PAIRS, 0, 0)  15.9 us
    all_to_all x1, blocking collectives, others(): parts = lax.all_to_all(parts, axis, 0, 0)  14.6 us
    all_gather x1, blocking collectives, on_device(): lax.all_gather(first.astype(jnp.bfloat16), 'yh')  13.6 us
    all_to_all x1, waiting for transfers between devices, others(): parts = lax.all_to_all(parts, axis, 0, 0)  6.77 us
  transfers between devices with their start and end apart: 4, of which 3 were waited for; matrix products, arithmetic and copies ran while one was open for 1% of the time, Pallas kernels for 0%

profile of v4, /device:TPU:1, one launch (start us, length us, event | category | flops | bytes accessed | tf_op | source)
XLA Modules:
  0.0 153.6 jit_solution(5900428285332837689)
XLA Ops:
  0.0 1.9 %broadcast_in_dim.12 = bf16[4,800,128]{2,1,0:T(8,128)(2,1)} broadcast(bf16[800,128]{1,0:T(8,128)(2,1)} %bitcast.115), dimensions={1,2} | broadcast | bytes 1024000 | tf_op jit(solution)/shard_map/broadcast_in_dim | solution.py:19
  1.9 5.0 %all-to-all-start = ((bf16[4,800,128]{2,1,0:T(8,128)(2,1)}), bf16[4,800,128]{2,1,0:T(8,128)(2,1)S(1)}, u32[]{:S(2)}, u32[]{:S(2)}) async-start(bf16[4,800,128]{2,1,0:T(8,128)(2,1)} %broadcast_in_dim.12), calls=%async_computation | async-start | bytes 1638400 | tf_op jit(solution)/shard_map/all_to_all | solution.py:19
  6.9 19.5 %all-gather = bf16[3200,128]{1,0:T(8,128)(2,1)S(1)} all-gather(bf16[800,128]{1,0:T(8,128)(2,1)S(1)} %bitcast.116), channel_id=2, replica_groups=mesh['yh'=4,'x'=4,'core'=2,'yl'=2,'zh'=4,'zl'=2] {'yh'}, dimensions={0}, use_global_device_ids=true | all-gather | bytes 1024000 | tf_op jit(solution)/shard_map/all_gather | solution.py:39
  26.4 6.9 %collective-permute-start = (bf16[4,800,128]{2,1,0:T(8,128)(2,1)S(1)}, bf16[4,800,128]{2,1,0:T(8,128)(2,1)S(1)}, u32[]{:S(2)}, u32[]{:S(2)}) collective-permute-start(bf16[4,800,128]{2,1,0:T(8,128)(2,1)S(1)} %bitcast.108), channel_id=1, source_target_pairs={{0,16},{16,0},{1,17},{17,1},{2,18},{18,2},{3,19},{19,3},{4,20},{20... | collective-permute-start | bytes 2457608 | tf_op jit(solution)/shard_map/ppermute | solution.py:34
  33.3 1.9 %collective-permute-done = bf16[4,800,128]{2,1,0:T(8,128)(2,1)S(1)} collective-permute-done((bf16[4,800,128]{2,1,0:T(8,128)(2,1)S(1)}, bf16[4,800,128]{2,1,0:T(8,128)(2,1)S(1)}, u32[]{:S(2)}, u32[]{:S(2)}) %collective-permute-start) | collective-permute-done | bytes 819232 | tf_op jit(solution)/shard_map/ppermute | solution.py:34
  35.3 1.3 fusion.12
  36.6 15.9 %all_to_all.35 = bf16[4,4,128,2,128]{2,4,3,1,0:T(8,128)(2,1)S(1)} all-to-all(bf16[4,4,128,2,128]{2,4,3,1,0:T(8,128)(2,1)S(1)} %copy.14), channel_id=1, replica_groups=mesh['yh'=4,'x'=4,'core'=2,'yl'=2,'zh'=4,'zl'=2] {'yl','zl'}, dimensions={0} | all-to-all | bytes 2097152 | tf_op jit(solution)/shard_map/all_to_all | solution.py:44
  52.5 0.2 convert_reduce_fusion
  52.7 17.7 %all_to_all.36 = bf16[4,128,2,128]{1,3,2,0:T(8,128)(2,1)S(1)} all-to-all(bf16[4,128,2,128]{1,3,2,0:T(8,128)(2,1)S(1)} %reduce-precision_convert_fusion), channel_id=1, replica_groups=mesh['yh'=4,'x'=4,'core'=2,'yl'=2,'zh'=4,'zl'=2] {'zh'}, dimensions={0} | all-to-all | bytes 524288 | tf_op jit(solution)/shard_map/all_to_all | solution.py:45
  70.7 12.1 %all_to_all.37 = bf16[4,128,2,128]{3,1,2,0:T(8,128)(2,1)S(1)} all-to-all(bf16[4,128,2,128]{3,1,2,0:T(8,128)(2,1)S(1)} %broadcast_in_dim.27), channel_id=1, replica_groups=mesh['yh'=4,'x'=4,'core'=2,'yl'=2,'zh'=4,'zl'=2] {'zh'}, dimensions={0} | all-to-all | bytes 524288 | tf_op jit(solution)/shard_map/all_to_all | solution.py:19
  82.8 0.2 broadcast_in_dim.28
  83.0 11.9 %all_to_all.38 = bf16[4,4,128,2,128]{4,2,3,1,0:T(8,128)(2,1)S(1)} all-to-all(bf16[4,4,128,2,128]{4,2,3,1,0:T(8,128)(2,1)S(1)} %broadcast_in_dim.28), channel_id=1, replica_groups=mesh['yh'=4,'x'=4,'core'=2,'yl'=2,'zh'=4,'zl'=2] {'yl','zl'}, dimensions={0} | all-to-all | bytes 2097152 | tf_op jit(solution)/shard_map/all_to_all | solution.py:19
  94.9 1.9 %fusion.15 = bf16[4,800,128]{2,1,0:T(8,128)(2,1)} fusion(bf16[4,4,128,2,128]{4,2,3,1,0:T(8,128)(2,1)S(1)} %all_to_all.38, bf16[4,1,800,128]{3,2,1,0:T(8,128)(2,1)S(1)} %bitcast.118, bf16[4,1,800,128]{3,2,1,0:T(8,128)(2,1)S(1)} %bitcast.110), kind=kOutput, calls=%fused_computation.15 | convolution fusion | flops 840089600 | bytes 3506176 | tf_op jit(solution)/shard_map/dfct,edsft->ecs/dot_general | solution.py:51
  96.9 4.0 %all-to-all-start.5 = ((bf16[4,800,128]{2,1,0:T(8,128)(2,1)}), bf16[4,800,128]{2,1,0:T(8,128)(2,1)S(1)}, u32[]{:S(2)}, u32[]{:S(2)}) async-start(bf16[4,800,128]{2,1,0:T(8,128)(2,1)} %fusion.15), calls=%async_computation.5 | async-start | bytes 1638400 | tf_op jit(solution)/shard_map/all_to_all | solution.py:23
  100.8 1.7 %convolution_bitcast_fusion.1 = f32[800,128]{1,0:T(8,128)S(1)} fusion(bf16[4,1,800,128]{3,2,1,0:T(8,128)(2,1)} %bitcast.119, bf16[4,1,800,128]{3,2,1,0:T(8,128)(2,1)S(1)} %bitcast.111, bf16[4,4,128,2,128]{4,2,3,1,0:T(8,128)(2,1)S(1)} %all_to_all.38, s32[]{:T(128)S(6)} %select_n.10), kind=kOutput, calls=%fused_computation.18 | convolution fusion | flops 210534400 | bytes 2310148 | tf_op jit(solution)/shard_map/dfct,edsft->ecs/dot_general | solution.py:51
  102.6 6.8 %all-to-all-done.5 = bf16[4,800,128]{2,1,0:T(8,128)(2,1)S(1)} async-done(((bf16[4,800,128]{2,1,0:T(8,128)(2,1)}), bf16[4,800,128]{2,1,0:T(8,128)(2,1)S(1)}, u32[]{:S(2)}, u32[]{:S(2)}) %all-to-all-start.5) | async-done | bytes 819232 | tf_op jit(solution)/shard_map/all_to_all | solution.py:23
  109.3 0.3 select_reduce_fusion.1
  109.6 13.6 %all-gather.1 = bf16[3200,128]{1,0:T(8,128)(2,1)S(1)} all-gather(bf16[800,128]{1,0:T(8,128)(2,1)S(1)} %fusion.31), channel_id=3, replica_groups=mesh['yh'=4,'x'=4,'core'=2,'yl'=2,'zh'=4,'zl'=2] {'yh'}, dimensions={0}, use_global_device_ids=true | all-gather | bytes 1024000 | tf_op jit(solution)/shard_map/all_gather | solution.py:58
  123.2 11.2 %collective-permute-start.1 = (bf16[4,800,128]{2,1,0:T(8,128)(2,1)S(1)}, bf16[4,800,128]{2,1,0:T(8,128)(2,1)S(1)}, u32[]{:S(2)}, u32[]{:S(2)}) collective-permute-start(bf16[4,800,128]{2,1,0:T(8,128)(2,1)S(1)} %bitcast.112), channel_id=1, source_target_pairs={{0,16},{16,0},{1,17},{17,1},{2,18},{18,2},{3,19},{19,3},{4,20},{20... | collective-permute-start | bytes 2457608 | tf_op jit(solution)/shard_map/ppermute | solution.py:34
  134.4 1.9 %collective-permute-done.1 = bf16[4,800,128]{2,1,0:T(8,128)(2,1)S(1)} collective-permute-done((bf16[4,800,128]{2,1,0:T(8,128)(2,1)S(1)}, bf16[4,800,128]{2,1,0:T(8,128)(2,1)S(1)}, u32[]{:S(2)}, u32[]{:S(2)}) %collective-permute-start.1) | collective-permute-done | bytes 819232 | tf_op jit(solution)/shard_map/ppermute | solution.py:34
  136.4 1.0 fusion.18
  137.4 14.6 %all_to_all.39 = bf16[4,800,128]{2,1,0:T(8,128)(2,1)S(1)} all-to-all(bf16[4,800,128]{2,1,0:T(8,128)(2,1)S(1)} %fusion.18), channel_id=1, replica_groups=mesh['yh'=4,'x'=4,'core'=2,'yl'=2,'zh'=4,'zl'=2] {'x'}, dimensions={0} | all-to-all | bytes 1638400 | tf_op jit(solution)/shard_map/all_to_all | solution.py:23
  152.0 0.2 select_reduce_fusion
  152.3 1.3 fusion.25
  (13 shorter events, 0.4 us)
Async XLA Ops:
  1.9 5.0 %copy-start = (bf16[128,800]{0,1:T(8,128)(2,1)S(1)}, bf16[128,800]{0,1:T(8,128)(2,1)}, u32[]{:S(2)}) copy-start(bf16[128,800]{0,1:T(8,128)(2,1)} %param.1) | copy-start | bytes 614404
  1.9 24.5 %all-to-all-start = ((bf16[4,800,128]{2,1,0:T(8,128)(2,1)}), bf16[4,800,128]{2,1,0:T(8,128)(2,1)S(1)}, u32[]{:S(2)}, u32[]{:S(2)}) async-start(bf16[4,800,128]{2,1,0:T(8,128)(2,1)} %broadcast_in_dim.12), calls=%async_computation | async-start | bytes 1638400 | tf_op jit(solution)/shard_map/all_to_all | solution.py:19
  26.4 8.8 %collective-permute-start = (bf16[4,800,128]{2,1,0:T(8,128)(2,1)S(1)}, bf16[4,800,128]{2,1,0:T(8,128)(2,1)S(1)}, u32[]{:S(2)}, u32[]{:S(2)}) collective-permute-start(bf16[4,800,128]{2,1,0:T(8,128)(2,1)S(1)} %bitcast.108), channel_id=1, source_target_pairs={{0,16},{16,0},{1,17},{17,1},{2,18},{18,2},{3,19},{19,3},{4,20},{20... | collective-permute-start | bytes 2457608 | tf_op jit(solution)/shard_map/ppermute | solution.py:34
  35.3 59.7 %copy-start.1 = (bf16[4,800,128]{2,1,0:T(8,128)(2,1)}, bf16[4,800,128]{2,1,0:T(8,128)(2,1)S(1)}, u32[]{:S(2)}) copy-start(bf16[4,800,128]{2,1,0:T(8,128)(2,1)S(1)} %collective-permute-done) | copy-start | bytes 2457604
  96.9 12.5 %all-to-all-start.5 = ((bf16[4,800,128]{2,1,0:T(8,128)(2,1)}), bf16[4,800,128]{2,1,0:T(8,128)(2,1)S(1)}, u32[]{:S(2)}, u32[]{:S(2)}) async-start(bf16[4,800,128]{2,1,0:T(8,128)(2,1)} %fusion.15), calls=%async_computation.5 | async-start | bytes 1638400 | tf_op jit(solution)/shard_map/all_to_all | solution.py:23
  123.2 13.1 %collective-permute-start.1 = (bf16[4,800,128]{2,1,0:T(8,128)(2,1)S(1)}, bf16[4,800,128]{2,1,0:T(8,128)(2,1)S(1)}, u32[]{:S(2)}, u32[]{:S(2)}) collective-permute-start(bf16[4,800,128]{2,1,0:T(8,128)(2,1)S(1)} %bitcast.112), channel_id=1, source_target_pairs={{0,16},{16,0},{1,17},{17,1},{2,18},{18,2},{3,19},{19,3},{4,20},{20... | collective-permute-start | bytes 2457608 | tf_op jit(solution)/shard_map/ppermute | solution.py:34

commit v5 on v4

--- a/solution.py
+++ b/solution.py
@@ -43,7 +43,7 @@
     gram = jnp.einsum("ecs,dfct->edsft", along, across, preferred_element_type=jnp.float32)
     gram = lax.all_to_all((gram / COLS).astype(jnp.bfloat16), PAIRS, 0, 0)
     gram = total(lax.all_to_all(total(gram), "zh", 0, 0))
-    gram = spread(spread(gram, "zh"), PAIRS)
+    gram = spread(lax.all_gather(gram, "zh"), PAIRS)
     mine_only = lax.dynamic_slice_in_dim(gram, lax.axis_index("x"), 1, 0)
 
     def product(columns):

time: 156 us -> 157 us (level); the launches traced: 154 us -> 157 us
  blocking collectives: 105 us -> 108 us
    all_gather x0 -> x1, blocking collectives: none -> 11.5 us  [on_device(): gram = spread(lax.all_gather(gram, 'zh'), PAIRS)]
    all_to_all x2 -> x1, blocking collectives: 24 us -> 13 us  [spread(): lax.all_to_all(jnp.broadcast_to(block[None], (4,) + block.shape), axes, 0...]
    all_gather x1, blocking collectives: 13.6 us -> 16 us  [on_device(): lax.all_gather(first.astype(jnp.bfloat16), 'yh')]
where the time goes in v5:
time: 157 us
  blocking collectives  108 us (69%)
  starting transfers between devices  26.9 us (17%)
  waiting for transfers between devices  10.6 us (7%)
  matrix products  7.29 us (5%)
  local copies, waits for them, and re-layouts  2.42 us (2%)
    all_gather x1, blocking collectives, on_device(): along, across = (spread(mine, 'x'), lax.all_gather(mine, 'yh'))  19.5 us
    ppermute x2, starting transfers between devices, both_cores(): return jnp.stack([blocks, lax.ppermute(blocks, 'core', SWAP)], axis=1)  17.9 us
    all_to_all x1, blocking collectives, on_device(): gram = total(lax.all_to_all(total(gram), 'zh', 0, 0))  17.7 us
    all_gather x1, blocking collectives, on_device(): lax.all_gather(first.astype(jnp.bfloat16), 'yh')  16 us
    all_to_all x1, blocking collectives, on_device(): gram = lax.all_to_all((gram / COLS).astype(jnp.bfloat16), PAIRS, 0, 0)  15.9 us
    all_to_all x1, blocking collectives, others(): parts = lax.all_to_all(parts, axis, 0, 0)  14.6 us
    all_to_all x1, blocking collectives, spread(): lax.all_to_all(jnp.broadcast_to(block[None], (4,) + block.shape), axes, 0...  13 us
    all_gather x1, blocking collectives, on_device(): gram = spread(lax.all_gather(gram, 'zh'), PAIRS)  11.5 us
  transfers between devices with their start and end apart: 4, of which 3 were waited for; matrix products, arithmetic and copies ran while one was open for 1% of the time, Pallas kernels for 0%

profile of v5, /device:TPU:1, one launch (start us, length us, event | category | flops | bytes accessed | tf_op | source)
XLA Modules:
  0.0 156.5 jit_solution(10004733492881190718)
XLA Ops:
  0.0 1.9 %broadcast_in_dim.19 = bf16[4,800,128]{2,1,0:T(8,128)(2,1)} broadcast(bf16[800,128]{1,0:T(8,128)(2,1)} %bitcast.117), dimensions={1,2} | broadcast | bytes 1024000 | tf_op jit(solution)/shard_map/broadcast_in_dim | solution.py:19
  1.9 5.0 %all-to-all-start = ((bf16[4,800,128]{2,1,0:T(8,128)(2,1)}), bf16[4,800,128]{2,1,0:T(8,128)(2,1)S(1)}, u32[]{:S(2)}, u32[]{:S(2)}) async-start(bf16[4,800,128]{2,1,0:T(8,128)(2,1)} %broadcast_in_dim.19), calls=%async_computation | async-start | bytes 1638400 | tf_op jit(solution)/shard_map/all_to_all | solution.py:19
  6.9 19.5 %all-gather = bf16[3200,128]{1,0:T(8,128)(2,1)S(1)} all-gather(bf16[800,128]{1,0:T(8,128)(2,1)S(1)} %bitcast.118), channel_id=2, replica_groups=mesh['yh'=4,'x'=4,'core'=2,'yl'=2,'zh'=4,'zl'=2] {'yh'}, dimensions={0}, use_global_device_ids=true | all-gather | bytes 1024000 | tf_op jit(solution)/shard_map/all_gather | solution.py:39
  26.4 6.9 %collective-permute-start = (bf16[4,800,128]{2,1,0:T(8,128)(2,1)S(1)}, bf16[4,800,128]{2,1,0:T(8,128)(2,1)S(1)}, u32[]{:S(2)}, u32[]{:S(2)}) collective-permute-start(bf16[4,800,128]{2,1,0:T(8,128)(2,1)S(1)} %bitcast.110), channel_id=1, source_target_pairs={{0,16},{16,0},{1,17},{17,1},{2,18},{18,2},{3,19},{19,3},{4,20},{20... | collective-permute-start | bytes 2457608 | tf_op jit(solution)/shard_map/ppermute | solution.py:34
  33.3 1.9 %collective-permute-done = bf16[4,800,128]{2,1,0:T(8,128)(2,1)S(1)} collective-permute-done((bf16[4,800,128]{2,1,0:T(8,128)(2,1)S(1)}, bf16[4,800,128]{2,1,0:T(8,128)(2,1)S(1)}, u32[]{:S(2)}, u32[]{:S(2)}) %collective-permute-start) | collective-permute-done | bytes 819232 | tf_op jit(solution)/shard_map/ppermute | solution.py:34
  35.3 1.3 fusion.12
  36.6 15.9 %all_to_all.30 = bf16[4,4,128,2,128]{2,4,3,1,0:T(8,128)(2,1)S(1)} all-to-all(bf16[4,4,128,2,128]{2,4,3,1,0:T(8,128)(2,1)S(1)} %copy.13), channel_id=1, replica_groups=mesh['yh'=4,'x'=4,'core'=2,'yl'=2,'zh'=4,'zl'=2] {'yl','zl'}, dimensions={0} | all-to-all | bytes 2097152 | tf_op jit(solution)/shard_map/all_to_all | solution.py:44
  52.7 17.7 %all_to_all.31 = bf16[4,128,2,128]{1,3,2,0:T(8,128)(2,1)S(1)} all-to-all(bf16[4,128,2,128]{1,3,2,0:T(8,128)(2,1)S(1)} %reduce-precision_convert_fusion), channel_id=1, replica_groups=mesh['yh'=4,'x'=4,'core'=2,'yl'=2,'zh'=4,'zl'=2] {'zh'}, dimensions={0} | all-to-all | bytes 524288 | tf_op jit(solution)/shard_map/all_to_all | solution.py:45
  70.5 11.5 %all-gather.1 = bf16[512,2,128]{0,2,1:T(8,128)(2,1)S(1)} all-gather(bf16[128,2,128]{0,2,1:T(8,128)(2,1)S(1)} %reduce-precision_convert_fusion.1), channel_id=3, replica_groups=mesh['yh'=4,'x'=4,'core'=2,'yl'=2,'zh'=4,'zl'=2] {'zh'}, dimensions={0}, use_global_device_ids=true | all-gather | bytes 327680 | tf_op jit(solution)/shard_map/all_gather | solution.py:46
  82.1 0.2 copy.15
  82.3 0.2 broadcast_in_dim.21
  82.5 13.0 %all_to_all.32 = bf16[4,4,128,2,128]{4,2,3,1,0:T(8,128)(2,1)S(1)} all-to-all(bf16[4,4,128,2,128]{4,2,3,1,0:T(8,128)(2,1)S(1)} %broadcast_in_dim.21), channel_id=1, replica_groups=mesh['yh'=4,'x'=4,'core'=2,'yl'=2,'zh'=4,'zl'=2] {'yl','zl'}, dimensions={0} | all-to-all | bytes 2097152 | tf_op jit(solution)/shard_map/all_to_all | solution.py:19
  95.5 1.9 %fusion.15 = bf16[4,800,128]{2,1,0:T(8,128)(2,1)} fusion(bf16[4,4,128,2,128]{4,2,3,1,0:T(8,128)(2,1)S(1)} %all_to_all.32, bf16[4,1,800,128]{3,2,1,0:T(8,128)(2,1)S(1)} %bitcast.120, bf16[4,1,800,128]{3,2,1,0:T(8,128)(2,1)S(1)} %bitcast.112), kind=kOutput, calls=%fused_computation.15 | convolution fusion | flops 840089600 | bytes 3506176 | tf_op jit(solution)/shard_map/dfct,edsft->ecs/dot_general | solution.py:51
  97.5 4.0 %all-to-all-start.4 = ((bf16[4,800,128]{2,1,0:T(8,128)(2,1)}), bf16[4,800,128]{2,1,0:T(8,128)(2,1)S(1)}, u32[]{:S(2)}, u32[]{:S(2)}) async-start(bf16[4,800,128]{2,1,0:T(8,128)(2,1)} %fusion.15), calls=%async_computation.4 | async-start | bytes 1638400 | tf_op jit(solution)/shard_map/all_to_all | solution.py:23
  101.4 1.7 %convolution_bitcast_fusion.1 = f32[800,128]{1,0:T(8,128)S(1)} fusion(bf16[4,1,800,128]{3,2,1,0:T(8,128)(2,1)} %bitcast.121, bf16[4,1,800,128]{3,2,1,0:T(8,128)(2,1)S(1)} %bitcast.113, bf16[4,4,128,2,128]{4,2,3,1,0:T(8,128)(2,1)S(1)} %all_to_all.32, s32[]{:T(128)S(6)} %select_n.10), kind=kOutput, calls=%fused_computation.18 | convolution fusion | flops 210534400 | bytes 2310148 | tf_op jit(solution)/shard_map/dfct,edsft->ecs/dot_general | solution.py:51
  103.2 6.8 %all-to-all-done.4 = bf16[4,800,128]{2,1,0:T(8,128)(2,1)S(1)} async-done(((bf16[4,800,128]{2,1,0:T(8,128)(2,1)}), bf16[4,800,128]{2,1,0:T(8,128)(2,1)S(1)}, u32[]{:S(2)}, u32[]{:S(2)}) %all-to-all-start.4) | async-done | bytes 819232 | tf_op jit(solution)/shard_map/all_to_all | solution.py:23
  110.0 0.3 select_reduce_fusion.1
  110.3 16.0 %all-gather.2 = bf16[3200,128]{1,0:T(8,128)(2,1)S(1)} all-gather(bf16[800,128]{1,0:T(8,128)(2,1)S(1)} %fusion.31), channel_id=4, replica_groups=mesh['yh'=4,'x'=4,'core'=2,'yl'=2,'zh'=4,'zl'=2] {'yh'}, dimensions={0}, use_global_device_ids=true | all-gather | bytes 1024000 | tf_op jit(solution)/shard_map/all_gather | solution.py:58
  126.3 11.0 %collective-permute-start.1 = (bf16[4,800,128]{2,1,0:T(8,128)(2,1)S(1)}, bf16[4,800,128]{2,1,0:T(8,128)(2,1)S(1)}, u32[]{:S(2)}, u32[]{:S(2)}) collective-permute-start(bf16[4,800,128]{2,1,0:T(8,128)(2,1)S(1)} %bitcast.114), channel_id=1, source_target_pairs={{0,16},{16,0},{1,17},{17,1},{2,18},{18,2},{3,19},{19,3},{4,20},{20... | collective-permute-start | bytes 2457608 | tf_op jit(solution)/shard_map/ppermute | solution.py:34
  137.3 1.9 %collective-permute-done.1 = bf16[4,800,128]{2,1,0:T(8,128)(2,1)S(1)} collective-permute-done((bf16[4,800,128]{2,1,0:T(8,128)(2,1)S(1)}, bf16[4,800,128]{2,1,0:T(8,128)(2,1)S(1)}, u32[]{:S(2)}, u32[]{:S(2)}) %collective-permute-start.1) | collective-permute-done | bytes 819232 | tf_op jit(solution)/shard_map/ppermute | solution.py:34
  139.3 1.0 fusion.18
  140.3 14.6 %all_to_all.33 = bf16[4,800,128]{2,1,0:T(8,128)(2,1)S(1)} all-to-all(bf16[4,800,128]{2,1,0:T(8,128)(2,1)S(1)} %fusion.18), channel_id=1, replica_groups=mesh['yh'=4,'x'=4,'core'=2,'yl'=2,'zh'=4,'zl'=2] {'x'}, dimensions={0} | all-to-all | bytes 1638400 | tf_op jit(solution)/shard_map/all_to_all | solution.py:23
  155.0 0.2 select_reduce_fusion
  155.2 1.3 fusion.25
  (13 shorter events, 0.4 us)
Async XLA Ops:
  1.9 5.0 %copy-start = (bf16[128,800]{0,1:T(8,128)(2,1)S(1)}, bf16[128,800]{0,1:T(8,128)(2,1)}, u32[]{:S(2)}) copy-start(bf16[128,800]{0,1:T(8,128)(2,1)} %param.1) | copy-start | bytes 614404
  1.9 24.5 %all-to-all-start = ((bf16[4,800,128]{2,1,0:T(8,128)(2,1)}), bf16[4,800,128]{2,1,0:T(8,128)(2,1)S(1)}, u32[]{:S(2)}, u32[]{:S(2)}) async-start(bf16[4,800,128]{2,1,0:T(8,128)(2,1)} %broadcast_in_dim.19), calls=%async_computation | async-start | bytes 1638400 | tf_op jit(solution)/shard_map/all_to_all | solution.py:19
  26.4 8.8 %collective-permute-start = (bf16[4,800,128]{2,1,0:T(8,128)(2,1)S(1)}, bf16[4,800,128]{2,1,0:T(8,128)(2,1)S(1)}, u32[]{:S(2)}, u32[]{:S(2)}) collective-permute-start(bf16[4,800,128]{2,1,0:T(8,128)(2,1)S(1)} %bitcast.110), channel_id=1, source_target_pairs={{0,16},{16,0},{1,17},{17,1},{2,18},{18,2},{3,19},{19,3},{4,20},{20... | collective-permute-start | bytes 2457608 | tf_op jit(solution)/shard_map/ppermute | solution.py:34
  35.3 60.3 %copy-start.1 = (bf16[4,800,128]{2,1,0:T(8,128)(2,1)}, bf16[4,800,128]{2,1,0:T(8,128)(2,1)S(1)}, u32[]{:S(2)}) copy-start(bf16[4,800,128]{2,1,0:T(8,128)(2,1)S(1)} %collective-permute-done) | copy-start | bytes 2457604
  97.5 12.5 %all-to-all-start.4 = ((bf16[4,800,128]{2,1,0:T(8,128)(2,1)}), bf16[4,800,128]{2,1,0:T(8,128)(2,1)S(1)}, u32[]{:S(2)}, u32[]{:S(2)}) async-start(bf16[4,800,128]{2,1,0:T(8,128)(2,1)} %fusion.15), calls=%async_computation.4 | async-start | bytes 1638400 | tf_op jit(solution)/shard_map/all_to_all | solution.py:23
  126.3 13.0 %collective-permute-start.1 = (bf16[4,800,128]{2,1,0:T(8,128)(2,1)S(1)}, bf16[4,800,128]{2,1,0:T(8,128)(2,1)S(1)}, u32[]{:S(2)}, u32[]{:S(2)}) collective-permute-start(bf16[4,800,128]{2,1,0:T(8,128)(2,1)S(1)} %bitcast.114), channel_id=1, source_target_pairs={{0,16},{16,0},{1,17},{17,1},{2,18},{18,2},{3,19},{19,3},{4,20},{20... | collective-permute-start | bytes 2457608 | tf_op jit(solution)/shard_map/ppermute | solution.py:34

commit v6 on v4

--- a/solution.py
+++ b/solution.py
@@ -11,7 +11,7 @@
 coef_quintic = 2.0315
 
 SPLIT = {"yh": 4, "x": 4, "core": 2, "yl": 2, "zh": 4, "zl": 2}
-PAIRS = ("yl", "zl")
+PAIRS = ("zl", "yl")
 SWAP = [(0, 1), (1, 0)]
 
 

time: 156 us -> 156 us (level); the launches traced: 154 us -> 155 us
  blocking collectives: 105 us -> 107 us
where the time goes in v6:
time: 156 us; the launch traced here: 155 us
  blocking collectives  107 us (69%)
  starting transfers between devices  27.4 us (18%)
  waiting for transfers between devices  10.6 us (7%)
  matrix products  7.29 us (5%)
  local copies, waits for them, and re-layouts  2.38 us (2%)
    all_to_all x2, blocking collectives, spread(): lax.all_to_all(jnp.broadcast_to(block[None], (4,) + block.shape), axes, 0...  24.4 us
    all_gather x1, blocking collectives, on_device(): along, across = (spread(mine, 'x'), lax.all_gather(mine, 'yh'))  19.5 us
    ppermute x2, starting transfers between devices, both_cores(): return jnp.stack([blocks, lax.ppermute(blocks, 'core', SWAP)], axis=1)  18.5 us
    all_to_all x1, blocking collectives, on_device(): gram = total(lax.all_to_all(total(gram), 'zh', 0, 0))  17.7 us
    all_to_all x1, blocking collectives, on_device(): gram = lax.all_to_all((gram / COLS).astype(jnp.bfloat16), PAIRS, 0, 0)  15.9 us
    all_to_all x1, blocking collectives, others(): parts = lax.all_to_all(parts, axis, 0, 0)  14.6 us
    all_gather x1, blocking collectives, on_device(): lax.all_gather(first.astype(jnp.bfloat16), 'yh')  14.5 us
    all_to_all x1, waiting for transfers between devices, others(): parts = lax.all_to_all(parts, axis, 0, 0)  6.77 us
  transfers between devices with their start and end apart: 4, of which 3 were waited for; matrix products, arithmetic and copies ran while one was open for 1% of the time, Pallas kernels for 0%

profile of v6, /device:TPU:1, one launch (start us, length us, event | category | flops | bytes accessed | tf_op | source)
XLA Modules:
  0.0 155.3 jit_solution(2000248038025654256)
XLA Ops:
  0.0 1.9 %broadcast_in_dim.12 = bf16[4,800,128]{2,1,0:T(8,128)(2,1)} broadcast(bf16[800,128]{1,0:T(8,128)(2,1)} %bitcast.115), dimensions={1,2} | broadcast | bytes 1024000 | tf_op jit(solution)/shard_map/broadcast_in_dim | solution.py:19
  1.9 5.0 %all-to-all-start = ((bf16[4,800,128]{2,1,0:T(8,128)(2,1)}), bf16[4,800,128]{2,1,0:T(8,128)(2,1)S(1)}, u32[]{:S(2)}, u32[]{:S(2)}) async-start(bf16[4,800,128]{2,1,0:T(8,128)(2,1)} %broadcast_in_dim.12), calls=%async_computation | async-start | bytes 1638400 | tf_op jit(solution)/shard_map/all_to_all | solution.py:19
  6.9 19.5 %all-gather = bf16[3200,128]{1,0:T(8,128)(2,1)S(1)} all-gather(bf16[800,128]{1,0:T(8,128)(2,1)S(1)} %bitcast.116), channel_id=2, replica_groups=mesh['yh'=4,'x'=4,'core'=2,'yl'=2,'zh'=4,'zl'=2] {'yh'}, dimensions={0}, use_global_device_ids=true | all-gather | bytes 1024000 | tf_op jit(solution)/shard_map/all_gather | solution.py:39
  26.4 6.9 %collective-permute-start = (bf16[4,800,128]{2,1,0:T(8,128)(2,1)S(1)}, bf16[4,800,128]{2,1,0:T(8,128)(2,1)S(1)}, u32[]{:S(2)}, u32[]{:S(2)}) collective-permute-start(bf16[4,800,128]{2,1,0:T(8,128)(2,1)S(1)} %bitcast.108), channel_id=1, source_target_pairs={{0,16},{16,0},{1,17},{17,1},{2,18},{18,2},{3,19},{19,3},{4,20},{20... | collective-permute-start | bytes 2457608 | tf_op jit(solution)/shard_map/ppermute | solution.py:34
  33.3 1.9 %collective-permute-done = bf16[4,800,128]{2,1,0:T(8,128)(2,1)S(1)} collective-permute-done((bf16[4,800,128]{2,1,0:T(8,128)(2,1)S(1)}, bf16[4,800,128]{2,1,0:T(8,128)(2,1)S(1)}, u32[]{:S(2)}, u32[]{:S(2)}) %collective-permute-start) | collective-permute-done | bytes 819232 | tf_op jit(solution)/shard_map/ppermute | solution.py:34
  35.3 1.3 fusion.12
  36.6 15.9 %all_to_all.35 = bf16[4,4,128,2,128]{2,4,3,1,0:T(8,128)(2,1)S(1)} all-to-all(bf16[4,4,128,2,128]{2,4,3,1,0:T(8,128)(2,1)S(1)} %copy.14), channel_id=1, replica_groups=mesh['yh'=4,'x'=4,'core'=2,'yl'=2,'zh'=4,'zl'=2] {'zl','yl'}, dimensions={0} | all-to-all | bytes 2097152 | tf_op jit(solution)/shard_map/all_to_all | solution.py:44
  52.5 0.2 convert_reduce_fusion
  52.7 17.7 %all_to_all.36 = bf16[4,128,2,128]{1,3,2,0:T(8,128)(2,1)S(1)} all-to-all(bf16[4,128,2,128]{1,3,2,0:T(8,128)(2,1)S(1)} %reduce-precision_convert_fusion), channel_id=1, replica_groups=mesh['yh'=4,'x'=4,'core'=2,'yl'=2,'zh'=4,'zl'=2] {'zh'}, dimensions={0} | all-to-all | bytes 524288 | tf_op jit(solution)/shard_map/all_to_all | solution.py:45
  70.7 12.1 %all_to_all.37 = bf16[4,128,2,128]{3,1,2,0:T(8,128)(2,1)S(1)} all-to-all(bf16[4,128,2,128]{3,1,2,0:T(8,128)(2,1)S(1)} %broadcast_in_dim.27), channel_id=1, replica_groups=mesh['yh'=4,'x'=4,'core'=2,'yl'=2,'zh'=4,'zl'=2] {'zh'}, dimensions={0} | all-to-all | bytes 524288 | tf_op jit(solution)/shard_map/all_to_all | solution.py:19
  82.8 0.2 broadcast_in_dim.28
  83.0 12.3 %all_to_all.38 = bf16[4,4,128,2,128]{4,2,3,1,0:T(8,128)(2,1)S(1)} all-to-all(bf16[4,4,128,2,128]{4,2,3,1,0:T(8,128)(2,1)S(1)} %broadcast_in_dim.28), channel_id=1, replica_groups=mesh['yh'=4,'x'=4,'core'=2,'yl'=2,'zh'=4,'zl'=2] {'zl','yl'}, dimensions={0} | all-to-all | bytes 2097152 | tf_op jit(solution)/shard_map/all_to_all | solution.py:19
  95.3 1.9 %fusion.15 = bf16[4,800,128]{2,1,0:T(8,128)(2,1)} fusion(bf16[4,4,128,2,128]{4,2,3,1,0:T(8,128)(2,1)S(1)} %all_to_all.38, bf16[4,1,800,128]{3,2,1,0:T(8,128)(2,1)S(1)} %bitcast.118, bf16[4,1,800,128]{3,2,1,0:T(8,128)(2,1)S(1)} %bitcast.110), kind=kOutput, calls=%fused_computation.15 | convolution fusion | flops 840089600 | bytes 3506176 | tf_op jit(solution)/shard_map/dfct,edsft->ecs/dot_general | solution.py:51
  97.3 4.0 %all-to-all-start.5 = ((bf16[4,800,128]{2,1,0:T(8,128)(2,1)}), bf16[4,800,128]{2,1,0:T(8,128)(2,1)S(1)}, u32[]{:S(2)}, u32[]{:S(2)}) async-start(bf16[4,800,128]{2,1,0:T(8,128)(2,1)} %fusion.15), calls=%async_computation.5 | async-start | bytes 1638400 | tf_op jit(solution)/shard_map/all_to_all | solution.py:23
  101.2 1.7 %convolution_bitcast_fusion.1 = f32[800,128]{1,0:T(8,128)S(1)} fusion(bf16[4,1,800,128]{3,2,1,0:T(8,128)(2,1)} %bitcast.119, bf16[4,1,800,128]{3,2,1,0:T(8,128)(2,1)S(1)} %bitcast.111, bf16[4,4,128,2,128]{4,2,3,1,0:T(8,128)(2,1)S(1)} %all_to_all.38, s32[]{:T(128)S(6)} %select_n.10), kind=kOutput, calls=%fused_computation.18 | convolution fusion | flops 210534400 | bytes 2310148 | tf_op jit(solution)/shard_map/dfct,edsft->ecs/dot_general | solution.py:51
  103.0 6.8 %all-to-all-done.5 = bf16[4,800,128]{2,1,0:T(8,128)(2,1)S(1)} async-done(((bf16[4,800,128]{2,1,0:T(8,128)(2,1)}), bf16[4,800,128]{2,1,0:T(8,128)(2,1)S(1)}, u32[]{:S(2)}, u32[]{:S(2)}) %all-to-all-start.5) | async-done | bytes 819232 | tf_op jit(solution)/shard_map/all_to_all | solution.py:23
  109.8 0.3 select_reduce_fusion.1
  110.1 14.5 %all-gather.1 = bf16[3200,128]{1,0:T(8,128)(2,1)S(1)} all-gather(bf16[800,128]{1,0:T(8,128)(2,1)S(1)} %fusion.31), channel_id=3, replica_groups=mesh['yh'=4,'x'=4,'core'=2,'yl'=2,'zh'=4,'zl'=2] {'yh'}, dimensions={0}, use_global_device_ids=true | all-gather | bytes 1024000 | tf_op jit(solution)/shard_map/all_gather | solution.py:58
  124.5 11.6 %collective-permute-start.1 = (bf16[4,800,128]{2,1,0:T(8,128)(2,1)S(1)}, bf16[4,800,128]{2,1,0:T(8,128)(2,1)S(1)}, u32[]{:S(2)}, u32[]{:S(2)}) collective-permute-start(bf16[4,800,128]{2,1,0:T(8,128)(2,1)S(1)} %bitcast.112), channel_id=1, source_target_pairs={{0,16},{16,0},{1,17},{17,1},{2,18},{18,2},{3,19},{19,3},{4,20},{20... | collective-permute-start | bytes 2457608 | tf_op jit(solution)/shard_map/ppermute | solution.py:34
  136.1 1.9 %collective-permute-done.1 = bf16[4,800,128]{2,1,0:T(8,128)(2,1)S(1)} collective-permute-done((bf16[4,800,128]{2,1,0:T(8,128)(2,1)S(1)}, bf16[4,800,128]{2,1,0:T(8,128)(2,1)S(1)}, u32[]{:S(2)}, u32[]{:S(2)}) %collective-permute-start.1) | collective-permute-done | bytes 819232 | tf_op jit(solution)/shard_map/ppermute | solution.py:34
  138.1 1.0 fusion.18
  139.1 14.6 %all_to_all.39 = bf16[4,800,128]{2,1,0:T(8,128)(2,1)S(1)} all-to-all(bf16[4,800,128]{2,1,0:T(8,128)(2,1)S(1)} %fusion.18), channel_id=1, replica_groups=mesh['yh'=4,'x'=4,'core'=2,'yl'=2,'zh'=4,'zl'=2] {'x'}, dimensions={0} | all-to-all | bytes 1638400 | tf_op jit(solution)/shard_map/all_to_all | solution.py:23
  153.8 0.2 select_reduce_fusion
  154.0 1.3 fusion.25
  (13 shorter events, 0.4 us)
Async XLA Ops:
  1.9 5.0 %copy-start = (bf16[128,800]{0,1:T(8,128)(2,1)S(1)}, bf16[128,800]{0,1:T(8,128)(2,1)}, u32[]{:S(2)}) copy-start(bf16[128,800]{0,1:T(8,128)(2,1)} %param.1) | copy-start | bytes 614404
  1.9 24.5 %all-to-all-start = ((bf16[4,800,128]{2,1,0:T(8,128)(2,1)}), bf16[4,800,128]{2,1,0:T(8,128)(2,1)S(1)}, u32[]{:S(2)}, u32[]{:S(2)}) async-start(bf16[4,800,128]{2,1,0:T(8,128)(2,1)} %broadcast_in_dim.12), calls=%async_computation | async-start | bytes 1638400 | tf_op jit(solution)/shard_map/all_to_all | solution.py:19
  26.4 8.8 %collective-permute-start = (bf16[4,800,128]{2,1,0:T(8,128)(2,1)S(1)}, bf16[4,800,128]{2,1,0:T(8,128)(2,1)S(1)}, u32[]{:S(2)}, u32[]{:S(2)}) collective-permute-start(bf16[4,800,128]{2,1,0:T(8,128)(2,1)S(1)} %bitcast.108), channel_id=1, source_target_pairs={{0,16},{16,0},{1,17},{17,1},{2,18},{18,2},{3,19},{19,3},{4,20},{20... | collective-permute-start | bytes 2457608 | tf_op jit(solution)/shard_map/ppermute | solution.py:34
  35.3 60.1 %copy-start.1 = (bf16[4,800,128]{2,1,0:T(8,128)(2,1)}, bf16[4,800,128]{2,1,0:T(8,128)(2,1)S(1)}, u32[]{:S(2)}) copy-start(bf16[4,800,128]{2,1,0:T(8,128)(2,1)S(1)} %collective-permute-done) | copy-start | bytes 2457604
  97.3 12.5 %all-to-all-start.5 = ((bf16[4,800,128]{2,1,0:T(8,128)(2,1)}), bf16[4,800,128]{2,1,0:T(8,128)(2,1)S(1)}, u32[]{:S(2)}, u32[]{:S(2)}) async-start(bf16[4,800,128]{2,1,0:T(8,128)(2,1)} %fusion.15), calls=%async_computation.5 | async-start | bytes 1638400 | tf_op jit(solution)/shard_map/all_to_all | solution.py:23
  124.5 13.5 %collective-permute-start.1 = (bf16[4,800,128]{2,1,0:T(8,128)(2,1)S(1)}, bf16[4,800,128]{2,1,0:T(8,128)(2,1)S(1)}, u32[]{:S(2)}, u32[]{:S(2)}) collective-permute-start(bf16[4,800,128]{2,1,0:T(8,128)(2,1)S(1)} %bitcast.112), channel_id=1, source_target_pairs={{0,16},{16,0},{1,17},{17,1},{2,18},{18,2},{3,19},{19,3},{4,20},{20... | collective-permute-start | bytes 2457608 | tf_op jit(solution)/shard_map/ppermute | solution.py:34

commit v7 on v4

--- a/solution.py
+++ b/solution.py
@@ -55,10 +55,11 @@
     parts, own = product(across)
     own = lax.optimization_barrier(own)
     first = lax.reduce_precision(own + others(parts, "x"), 8, 7)
-    parts, own = product(both_cores(lax.all_gather(first.astype(jnp.bfloat16), "yh")))
-    second = own + others(parts, "x")
-
-    updated = coef_linear * mine.astype(jnp.float32) + coef_cubic * first + coef_quintic * second
+    blocks = lax.all_gather(first.astype(jnp.bfloat16), "yh")
+    known = coef_linear * mine.astype(jnp.float32) + coef_cubic * first
+    partner, known = lax.optimization_barrier((lax.ppermute(blocks, "core", SWAP), known))
+    parts, own = product(jnp.stack([blocks, partner], axis=1))
+    updated = known + coef_quintic * (own + others(parts, "x"))
     return updated.astype(jnp.bfloat16).T
 
 

time: 156 us -> 156 us (level)
    ppermute x0 -> x1, starting transfers between devices: none -> 11.3 us  [on_device(): lax.ppermute(blocks, 'core', SWAP)]
    ppermute x2 -> x1, starting transfers between devices: 18.1 us -> 6.9 us  [both_cores(): return jnp.stack([blocks, lax.ppermute(blocks, 'core', SWAP)], axis=1)]
    ppermute x2 -> x1, waiting for transfers between devices: 3.87 us -> 1.94 us  [both_cores(): return jnp.stack([blocks, lax.ppermute(blocks, 'core', SWAP)], axis=1)]
    ppermute x0 -> x1, waiting for transfers between devices: none -> 1.94 us  [on_device(): lax.ppermute(blocks, 'core', SWAP)]
where the time goes in v7:
time: 156 us; the launch traced here: 154 us
  blocking collectives  105 us (67%)
  starting transfers between devices  27.1 us (17%)
  waiting for transfers between devices  10.6 us (7%)
  matrix products  6.6 us (4%)
  local copies, waits for them, and re-layouts  2.38 us (2%)
  other arithmetic  1.59 us (1%)
    all_to_all x2, blocking collectives, spread(): lax.all_to_all(jnp.broadcast_to(block[None], (4,) + block.shape), axes, 0...  24 us
    all_gather x1, blocking collectives, on_device(): along, across = (spread(mine, 'x'), lax.all_gather(mine, 'yh'))  19.5 us
    all_to_all x1, blocking collectives, on_device(): gram = total(lax.all_to_all(total(gram), 'zh', 0, 0))  17.7 us
    all_to_all x1, blocking collectives, on_device(): gram = lax.all_to_all((gram / COLS).astype(jnp.bfloat16), PAIRS, 0, 0)  15.9 us
    all_to_all x1, blocking collectives, others(): parts = lax.all_to_all(parts, axis, 0, 0)  14.6 us
    all_gather x1, blocking collectives, on_device(): blocks = lax.all_gather(first.astype(jnp.bfloat16), 'yh')  13.5 us
    ppermute x1, starting transfers between devices, on_device(): lax.ppermute(blocks, 'core', SWAP)  11.3 us
    ppermute x1, starting transfers between devices, both_cores(): return jnp.stack([blocks, lax.ppermute(blocks, 'core', SWAP)], axis=1)  6.9 us
  transfers between devices with their start and end apart: 4, of which 3 were waited for; matrix products, arithmetic and copies ran while one was open for 1% of the time, Pallas kernels for 0%

profile of v7, /device:TPU:1, one launch (start us, length us, event | category | flops | bytes accessed | tf_op | source)
XLA Modules:
  0.0 153.7 jit_solution(8844597295016544621)
XLA Ops:
  0.0 1.9 %broadcast_in_dim.12 = bf16[4,800,128]{2,1,0:T(8,128)(2,1)} broadcast(bf16[800,128]{1,0:T(8,128)(2,1)} %bitcast.102), dimensions={1,2} | broadcast | bytes 1024000 | tf_op jit(solution)/shard_map/broadcast_in_dim | solution.py:19
  1.9 5.0 %all-to-all-start = ((bf16[4,800,128]{2,1,0:T(8,128)(2,1)}), bf16[4,800,128]{2,1,0:T(8,128)(2,1)S(1)}, u32[]{:S(2)}, u32[]{:S(2)}) async-start(bf16[4,800,128]{2,1,0:T(8,128)(2,1)} %broadcast_in_dim.12), calls=%async_computation | async-start | bytes 1638400 | tf_op jit(solution)/shard_map/all_to_all | solution.py:19
  6.9 19.5 %all-gather = bf16[3200,128]{1,0:T(8,128)(2,1)S(1)} all-gather(bf16[800,128]{1,0:T(8,128)(2,1)S(1)} %bitcast.103), channel_id=2, replica_groups=mesh['yh'=4,'x'=4,'core'=2,'yl'=2,'zh'=4,'zl'=2] {'yh'}, dimensions={0}, use_global_device_ids=true | all-gather | bytes 1024000 | tf_op jit(solution)/shard_map/all_gather | solution.py:39
  26.4 6.9 %collective-permute-start = (bf16[4,800,128]{2,1,0:T(8,128)(2,1)S(1)}, bf16[4,800,128]{2,1,0:T(8,128)(2,1)S(1)}, u32[]{:S(2)}, u32[]{:S(2)}) collective-permute-start(bf16[4,800,128]{2,1,0:T(8,128)(2,1)S(1)} %bitcast.104), channel_id=1, source_target_pairs={{0,16},{16,0},{1,17},{17,1},{2,18},{18,2},{3,19},{19,3},{4,20},{20... | collective-permute-start | bytes 2457608 | tf_op jit(solution)/shard_map/ppermute | solution.py:34
  33.3 1.9 %collective-permute-done = bf16[4,800,128]{2,1,0:T(8,128)(2,1)S(1)} collective-permute-done((bf16[4,800,128]{2,1,0:T(8,128)(2,1)S(1)}, bf16[4,800,128]{2,1,0:T(8,128)(2,1)S(1)}, u32[]{:S(2)}, u32[]{:S(2)}) %collective-permute-start) | collective-permute-done | bytes 819232 | tf_op jit(solution)/shard_map/ppermute | solution.py:34
  35.3 1.3 fusion.12
  36.6 15.9 %all_to_all.35 = bf16[4,4,128,2,128]{2,4,3,1,0:T(8,128)(2,1)S(1)} all-to-all(bf16[4,4,128,2,128]{2,4,3,1,0:T(8,128)(2,1)S(1)} %copy.14), channel_id=1, replica_groups=mesh['yh'=4,'x'=4,'core'=2,'yl'=2,'zh'=4,'zl'=2] {'yl','zl'}, dimensions={0} | all-to-all | bytes 2097152 | tf_op jit(solution)/shard_map/all_to_all | solution.py:44
  52.7 17.7 %all_to_all.36 = bf16[4,128,2,128]{1,3,2,0:T(8,128)(2,1)S(1)} all-to-all(bf16[4,128,2,128]{1,3,2,0:T(8,128)(2,1)S(1)} %reduce-precision_convert_fusion), channel_id=1, replica_groups=mesh['yh'=4,'x'=4,'core'=2,'yl'=2,'zh'=4,'zl'=2] {'zh'}, dimensions={0} | all-to-all | bytes 524288 | tf_op jit(solution)/shard_map/all_to_all | solution.py:45
  70.7 12.1 %all_to_all.37 = bf16[4,128,2,128]{3,1,2,0:T(8,128)(2,1)S(1)} all-to-all(bf16[4,128,2,128]{3,1,2,0:T(8,128)(2,1)S(1)} %broadcast_in_dim.27), channel_id=1, replica_groups=mesh['yh'=4,'x'=4,'core'=2,'yl'=2,'zh'=4,'zl'=2] {'zh'}, dimensions={0} | all-to-all | bytes 524288 | tf_op jit(solution)/shard_map/all_to_all | solution.py:19
  82.8 0.2 broadcast_in_dim.28
  83.0 11.9 %all_to_all.38 = bf16[4,4,128,2,128]{4,2,3,1,0:T(8,128)(2,1)S(1)} all-to-all(bf16[4,4,128,2,128]{4,2,3,1,0:T(8,128)(2,1)S(1)} %broadcast_in_dim.28), channel_id=1, replica_groups=mesh['yh'=4,'x'=4,'core'=2,'yl'=2,'zh'=4,'zl'=2] {'yl','zl'}, dimensions={0} | all-to-all | bytes 2097152 | tf_op jit(solution)/shard_map/all_to_all | solution.py:19
  94.9 1.9 %fusion.15 = bf16[4,800,128]{2,1,0:T(8,128)(2,1)} fusion(bf16[4,4,128,2,128]{4,2,3,1,0:T(8,128)(2,1)S(1)} %all_to_all.38, bf16[4,1,800,128]{3,2,1,0:T(8,128)(2,1)S(1)} %bitcast.112, bf16[4,1,800,128]{3,2,1,0:T(8,128)(2,1)S(1)} %bitcast.106), kind=kOutput, calls=%fused_computation.15 | convolution fusion | flops 840089600 | bytes 3506176 | tf_op jit(solution)/shard_map/dfct,edsft->ecs/dot_general | solution.py:51
  96.9 4.0 %all-to-all-start.5 = ((bf16[4,800,128]{2,1,0:T(8,128)(2,1)}), bf16[4,800,128]{2,1,0:T(8,128)(2,1)S(1)}, u32[]{:S(2)}, u32[]{:S(2)}) async-start(bf16[4,800,128]{2,1,0:T(8,128)(2,1)} %fusion.15), calls=%async_computation.5 | async-start | bytes 1638400 | tf_op jit(solution)/shard_map/all_to_all | solution.py:23
  100.8 1.7 %convolution_bitcast_fusion.1 = f32[800,128]{1,0:T(8,128)S(1)} fusion(bf16[4,1,800,128]{3,2,1,0:T(8,128)(2,1)} %bitcast.113, bf16[4,1,800,128]{3,2,1,0:T(8,128)(2,1)S(1)} %bitcast.107, bf16[4,4,128,2,128]{4,2,3,1,0:T(8,128)(2,1)S(1)} %all_to_all.38, s32[]{:T(128)S(6)} %select_n.10), kind=kOutput, calls=%fused_computation.18 | convolution fusion | flops 210534400 | bytes 2310148 | tf_op jit(solution)/shard_map/dfct,edsft->ecs/dot_general | solution.py:51
  102.6 6.8 %all-to-all-done.5 = bf16[4,800,128]{2,1,0:T(8,128)(2,1)S(1)} async-done(((bf16[4,800,128]{2,1,0:T(8,128)(2,1)}), bf16[4,800,128]{2,1,0:T(8,128)(2,1)S(1)}, u32[]{:S(2)}, u32[]{:S(2)}) %all-to-all-start.5) | async-done | bytes 819232 | tf_op jit(solution)/shard_map/all_to_all | solution.py:23
  109.3 0.3 select_reduce_fusion.1
  109.7 13.5 %all-gather.1 = bf16[3200,128]{1,0:T(8,128)(2,1)S(1)} all-gather(bf16[800,128]{1,0:T(8,128)(2,1)S(1)} %get-tuple-element.14), channel_id=3, replica_groups=mesh['yh'=4,'x'=4,'core'=2,'yl'=2,'zh'=4,'zl'=2] {'yh'}, dimensions={0}, use_global_device_ids=true | all-gather | bytes 1024000 | tf_op jit(solution)/shard_map/all_gather | solution.py:58
  123.2 11.3 %collective-permute-start.1 = (bf16[4,800,128]{2,1,0:T(8,128)(2,1)S(1)}, bf16[4,800,128]{2,1,0:T(8,128)(2,1)S(1)}, u32[]{:S(2)}, u32[]{:S(2)}) collective-permute-start(bf16[4,800,128]{2,1,0:T(8,128)(2,1)S(1)} %bitcast.108), channel_id=1, source_target_pairs={{0,16},{16,0},{1,17},{17,1},{2,18},{18,2},{3,19},{19,3},{4,20},{20... | collective-permute-start | bytes 2457608 | tf_op jit(solution)/shard_map/ppermute | solution.py:60
  134.5 1.9 %collective-permute-done.1 = bf16[4,800,128]{2,1,0:T(8,128)(2,1)S(1)} collective-permute-done((bf16[4,800,128]{2,1,0:T(8,128)(2,1)S(1)}, bf16[4,800,128]{2,1,0:T(8,128)(2,1)S(1)}, u32[]{:S(2)}, u32[]{:S(2)}) %collective-permute-start.1) | collective-permute-done | bytes 819232 | tf_op jit(solution)/shard_map/ppermute | solution.py:60
  136.4 1.0 fusion.18
  137.5 14.6 %all_to_all.39 = bf16[4,800,128]{2,1,0:T(8,128)(2,1)S(1)} all-to-all(bf16[4,800,128]{2,1,0:T(8,128)(2,1)S(1)} %fusion.18), channel_id=1, replica_groups=mesh['yh'=4,'x'=4,'core'=2,'yl'=2,'zh'=4,'zl'=2] {'x'}, dimensions={0} | all-to-all | bytes 1638400 | tf_op jit(solution)/shard_map/all_to_all | solution.py:23
  152.1 0.2 select_reduce_fusion
  152.4 0.6 fusion.22
  153.0 0.7 fusion.28
  (14 shorter events, 0.6 us)
Async XLA Ops:
  1.9 5.0 %copy-start = (bf16[128,800]{0,1:T(8,128)(2,1)S(1)}, bf16[128,800]{0,1:T(8,128)(2,1)}, u32[]{:S(2)}) copy-start(bf16[128,800]{0,1:T(8,128)(2,1)} %param.1) | copy-start | bytes 614404
  1.9 24.5 %all-to-all-start = ((bf16[4,800,128]{2,1,0:T(8,128)(2,1)}), bf16[4,800,128]{2,1,0:T(8,128)(2,1)S(1)}, u32[]{:S(2)}, u32[]{:S(2)}) async-start(bf16[4,800,128]{2,1,0:T(8,128)(2,1)} %broadcast_in_dim.12), calls=%async_computation | async-start | bytes 1638400 | tf_op jit(solution)/shard_map/all_to_all | solution.py:19
  26.4 8.8 %collective-permute-start = (bf16[4,800,128]{2,1,0:T(8,128)(2,1)S(1)}, bf16[4,800,128]{2,1,0:T(8,128)(2,1)S(1)}, u32[]{:S(2)}, u32[]{:S(2)}) collective-permute-start(bf16[4,800,128]{2,1,0:T(8,128)(2,1)S(1)} %bitcast.104), channel_id=1, source_target_pairs={{0,16},{16,0},{1,17},{17,1},{2,18},{18,2},{3,19},{19,3},{4,20},{20... | collective-permute-start | bytes 2457608 | tf_op jit(solution)/shard_map/ppermute | solution.py:34
  35.3 59.7 %copy-start.1 = (bf16[4,800,128]{2,1,0:T(8,128)(2,1)}, bf16[4,800,128]{2,1,0:T(8,128)(2,1)S(1)}, u32[]{:S(2)}) copy-start(bf16[4,800,128]{2,1,0:T(8,128)(2,1)S(1)} %collective-permute-done) | copy-start | bytes 2457604
  96.9 12.5 %all-to-all-start.5 = ((bf16[4,800,128]{2,1,0:T(8,128)(2,1)}), bf16[4,800,128]{2,1,0:T(8,128)(2,1)S(1)}, u32[]{:S(2)}, u32[]{:S(2)}) async-start(bf16[4,800,128]{2,1,0:T(8,128)(2,1)} %fusion.15), calls=%async_computation.5 | async-start | bytes 1638400 | tf_op jit(solution)/shard_map/all_to_all | solution.py:23
  123.2 13.2 %collective-permute-start.1 = (bf16[4,800,128]{2,1,0:T(8,128)(2,1)S(1)}, bf16[4,800,128]{2,1,0:T(8,128)(2,1)S(1)}, u32[]{:S(2)}, u32[]{:S(2)}) collective-permute-start(bf16[4,800,128]{2,1,0:T(8,128)(2,1)S(1)} %bitcast.108), channel_id=1, source_target_pairs={{0,16},{16,0},{1,17},{17,1},{2,18},{18,2},{3,19},{19,3},{4,20},{20... | collective-permute-start | bytes 2457608 | tf_op jit(solution)/shard_map/ppermute | solution.py:60

commit v8 on v7

--- a/solution.py
+++ b/solution.py
@@ -57,8 +57,17 @@
     first = lax.reduce_precision(own + others(parts, "x"), 8, 7)
     blocks = lax.all_gather(first.astype(jnp.bfloat16), "yh")
     known = coef_linear * mine.astype(jnp.float32) + coef_cubic * first
-    partner, known = lax.optimization_barrier((lax.ppermute(blocks, "core", SWAP), known))
-    parts, own = product(jnp.stack([blocks, partner], axis=1))
+    def share(columns, f, rows):
+        return jnp.einsum(
+            "dct,edst->ecs", columns, rows[:, :, :, f], preferred_element_type=jnp.float32
+        )
+
+    partner = lax.ppermute(blocks, "core", SWAP)
+    near, near_own = share(blocks, 0, gram), share(blocks, 0, mine_only)[0]
+    known = known + coef_quintic * near_own
+    partner, near, known = lax.optimization_barrier((partner, near, known))
+    parts = (near + share(partner, 1, gram)).astype(jnp.bfloat16)
+    own = share(partner, 1, mine_only)[0]
     updated = known + coef_quintic * (own + others(parts, "x"))
     return updated.astype(jnp.bfloat16).T
 

time: 156 us -> 157 us (level)
  blocking collectives: 105 us -> 90.7 us
  waiting for transfers between devices: 10.6 us -> 21.9 us
  starting transfers between devices: 27.1 us -> 30.4 us
    all_to_all x1 -> x0, blocking collectives: 14.6 us -> none  [others(): parts = lax.all_to_all(parts, axis, 0, 0)]
    all_to_all x1 -> x2, waiting for transfers between devices: 6.77 us -> 19.1 us  [others(): parts = lax.all_to_all(parts, axis, 0, 0)]
    all_to_all x1 -> x2, starting transfers between devices: 3.97 us -> 7.47 us  [others(): parts = lax.all_to_all(parts, axis, 0, 0)]
    dot_general x0 -> x4, matrix products: none -> 2.01 us  [share(): jnp.einsum('dct,edst->ecs', columns, rows[:, :, :, f], preferred_element_...]
    dot_general x4 -> x2, matrix products: 5.32 us -> 3.68 us  [part(): jnp.einsum('dfct,edsft->ecs', columns, rows, preferred_element_type=jnp.f...]
  transfers between devices with their start and end apart: 4 -> 5, of which waited for: 3 -> 4; matrix products, arithmetic and copies ran while one was open for 1% -> 2% of each run, Pallas kernels for 0% -> 0%
where the time goes in v8:
time: 157 us; the launch traced here: 155 us
  blocking collectives  90.7 us (58%)
  starting transfers between devices  30.4 us (19%)
  waiting for transfers between devices  21.9 us (14%)
  matrix products  6.96 us (4%)
  local copies, waits for them, and re-layouts  2.58 us (2%)
  other arithmetic  2.57 us (2%)
    all_to_all x2, blocking collectives, spread(): lax.all_to_all(jnp.broadcast_to(block[None], (4,) + block.shape), axes, 0...  24 us
    all_gather x1, blocking collectives, on_device(): along, across = (spread(mine, 'x'), lax.all_gather(mine, 'yh'))  19.5 us
    all_to_all x2, waiting for transfers between devices, others(): parts = lax.all_to_all(parts, axis, 0, 0)  19.1 us
    all_to_all x1, blocking collectives, on_device(): gram = total(lax.all_to_all(total(gram), 'zh', 0, 0))  17.7 us
    all_to_all x1, blocking collectives, on_device(): gram = lax.all_to_all((gram / COLS).astype(jnp.bfloat16), PAIRS, 0, 0)  15.9 us
    all_gather x1, blocking collectives, on_device(): blocks = lax.all_gather(first.astype(jnp.bfloat16), 'yh')  13.6 us
    ppermute x1, starting transfers between devices, on_device(): partner = lax.ppermute(blocks, 'core', SWAP)  11.2 us
    all_to_all x2, starting transfers between devices, others(): parts = lax.all_to_all(parts, axis, 0, 0)  7.47 us
  transfers between devices with their start and end apart: 5, of which 4 were waited for; matrix products, arithmetic and copies ran while one was open for 2% of the time, Pallas kernels for 0%

profile of v8, /device:TPU:1, one launch (start us, length us, event | category | flops | bytes accessed | tf_op | source)
XLA Modules:
  0.0 155.2 jit_solution(16733777214291786766)
XLA Ops:
  0.0 2.0 %broadcast_in_dim.12 = bf16[4,800,128]{2,1,0:T(8,128)(2,1)} broadcast(bf16[800,128]{1,0:T(8,128)(2,1)} %bitcast.128), dimensions={1,2} | broadcast | bytes 1024000 | tf_op jit(solution)/shard_map/broadcast_in_dim | solution.py:19
  2.0 4.8 %all-to-all-start = ((bf16[4,800,128]{2,1,0:T(8,128)(2,1)}), bf16[4,800,128]{2,1,0:T(8,128)(2,1)S(1)}, u32[]{:S(2)}, u32[]{:S(2)}) async-start(bf16[4,800,128]{2,1,0:T(8,128)(2,1)} %broadcast_in_dim.12), calls=%async_computation | async-start | bytes 1638400 | tf_op jit(solution)/shard_map/all_to_all | solution.py:19
  6.8 19.5 %all-gather = bf16[3200,128]{1,0:T(8,128)(2,1)S(1)} all-gather(bf16[800,128]{1,0:T(8,128)(2,1)S(1)} %bitcast.129), channel_id=2, replica_groups=mesh['yh'=4,'x'=4,'core'=2,'yl'=2,'zh'=4,'zl'=2] {'yh'}, dimensions={0}, use_global_device_ids=true | all-gather | bytes 1024000 | tf_op jit(solution)/shard_map/all_gather | solution.py:39
  26.3 6.9 %collective-permute-start = (bf16[4,800,128]{2,1,0:T(8,128)(2,1)S(1)}, bf16[4,800,128]{2,1,0:T(8,128)(2,1)S(1)}, u32[]{:S(2)}, u32[]{:S(2)}) collective-permute-start(bf16[4,800,128]{2,1,0:T(8,128)(2,1)S(1)} %bitcast.130), channel_id=1, source_target_pairs={{0,16},{16,0},{1,17},{17,1},{2,18},{18,2},{3,19},{19,3},{4,20},{20... | collective-permute-start | bytes 2457608 | tf_op jit(solution)/shard_map/ppermute | solution.py:34
  33.3 1.9 %collective-permute-done = bf16[4,800,128]{2,1,0:T(8,128)(2,1)S(1)} collective-permute-done((bf16[4,800,128]{2,1,0:T(8,128)(2,1)S(1)}, bf16[4,800,128]{2,1,0:T(8,128)(2,1)S(1)}, u32[]{:S(2)}, u32[]{:S(2)}) %collective-permute-start) | collective-permute-done | bytes 819232 | tf_op jit(solution)/shard_map/ppermute | solution.py:34
  35.2 1.3 fusion.9
  36.6 15.9 %all_to_all.35 = bf16[4,4,128,2,128]{2,4,3,1,0:T(8,128)(2,1)S(1)} all-to-all(bf16[4,4,128,2,128]{2,4,3,1,0:T(8,128)(2,1)S(1)} %copy.13), channel_id=1, replica_groups=mesh['yh'=4,'x'=4,'core'=2,'yl'=2,'zh'=4,'zl'=2] {'yl','zl'}, dimensions={0} | all-to-all | bytes 2097152 | tf_op jit(solution)/shard_map/all_to_all | solution.py:44
  52.7 17.7 %all_to_all.36 = bf16[4,128,2,128]{1,3,2,0:T(8,128)(2,1)S(1)} all-to-all(bf16[4,128,2,128]{1,3,2,0:T(8,128)(2,1)S(1)} %reduce-precision_convert_fusion), channel_id=1, replica_groups=mesh['yh'=4,'x'=4,'core'=2,'yl'=2,'zh'=4,'zl'=2] {'zh'}, dimensions={0} | all-to-all | bytes 524288 | tf_op jit(solution)/shard_map/all_to_all | solution.py:45
  70.7 12.1 %all_to_all.37 = bf16[4,128,2,128]{3,1,2,0:T(8,128)(2,1)S(1)} all-to-all(bf16[4,128,2,128]{3,1,2,0:T(8,128)(2,1)S(1)} %broadcast_in_dim.27), channel_id=1, replica_groups=mesh['yh'=4,'x'=4,'core'=2,'yl'=2,'zh'=4,'zl'=2] {'zh'}, dimensions={0} | all-to-all | bytes 524288 | tf_op jit(solution)/shard_map/all_to_all | solution.py:19
  83.0 11.9 %all_to_all.38 = bf16[4,4,128,2,128]{4,2,3,1,0:T(8,128)(2,1)S(1)} all-to-all(bf16[4,4,128,2,128]{4,2,3,1,0:T(8,128)(2,1)S(1)} %broadcast_in_dim.28), channel_id=1, replica_groups=mesh['yh'=4,'x'=4,'core'=2,'yl'=2,'zh'=4,'zl'=2] {'yl','zl'}, dimensions={0} | all-to-all | bytes 2097152 | tf_op jit(solution)/shard_map/all_to_all | solution.py:19
  94.9 1.9 %fusion.12 = bf16[4,800,128]{2,1,0:T(8,128)(2,1)} fusion(bf16[4,4,128,2,128]{4,2,3,1,0:T(8,128)(2,1)S(1)} %all_to_all.38, bf16[4,1,800,128]{3,2,1,0:T(8,128)(2,1)S(1)} %bitcast.135, bf16[4,1,800,128]{3,2,1,0:T(8,128)(2,1)S(1)} %bitcast.132), kind=kOutput, calls=%fused_computation.14 | convolution fusion | flops 840089600 | bytes 3506176 | tf_op jit(solution)/shard_map/dfct,edsft->ecs/dot_general | solution.py:51
  96.8 4.0 %all-to-all-start.5 = ((bf16[4,800,128]{2,1,0:T(8,128)(2,1)}), bf16[4,800,128]{2,1,0:T(8,128)(2,1)S(1)}, u32[]{:S(2)}, u32[]{:S(2)}) async-start(bf16[4,800,128]{2,1,0:T(8,128)(2,1)} %fusion.12), calls=%async_computation.5 | async-start | bytes 1638400 | tf_op jit(solution)/shard_map/all_to_all | solution.py:23
  100.8 1.7 %convolution_bitcast_fusion.1 = f32[800,128]{1,0:T(8,128)S(1)} fusion(bf16[4,1,800,128]{3,2,1,0:T(8,128)(2,1)} %bitcast.136, bf16[4,1,800,128]{3,2,1,0:T(8,128)(2,1)S(1)} %bitcast.133, bf16[4,4,128,2,128]{4,2,3,1,0:T(8,128)(2,1)S(1)} %all_to_all.38, s32[]{:T(128)S(6)} %select_n.10), kind=kOutput, calls=%fused_computation.15 | convolution fusion | flops 210534400 | bytes 2310148 | tf_op jit(solution)/shard_map/dfct,edsft->ecs/dot_general | solution.py:51
  102.5 6.8 %all-to-all-done.5 = bf16[4,800,128]{2,1,0:T(8,128)(2,1)S(1)} async-done(((bf16[4,800,128]{2,1,0:T(8,128)(2,1)}), bf16[4,800,128]{2,1,0:T(8,128)(2,1)S(1)}, u32[]{:S(2)}, u32[]{:S(2)}) %all-to-all-start.5) | async-done | bytes 819232 | tf_op jit(solution)/shard_map/all_to_all | solution.py:23
  109.6 13.6 %all-gather.1 = bf16[3200,128]{1,0:T(8,128)(2,1)S(1)} all-gather(bf16[800,128]{1,0:T(8,128)(2,1)S(1)} %fusion.26), channel_id=3, replica_groups=mesh['yh'=4,'x'=4,'core'=2,'yl'=2,'zh'=4,'zl'=2] {'yh'}, dimensions={0}, use_global_device_ids=true | all-gather | bytes 1024000 | tf_op jit(solution)/shard_map/all_gather | solution.py:58
  123.2 11.2 %collective-permute-start.1 = (bf16[4,800,128]{2,1,0:T(8,128)(2,1)S(1)}, bf16[4,800,128]{2,1,0:T(8,128)(2,1)S(1)}, u32[]{:S(2)}, u32[]{:S(2)}) collective-permute-start(bf16[4,800,128]{2,1,0:T(8,128)(2,1)S(1)} %bitcast.125), channel_id=1, source_target_pairs={{0,16},{16,0},{1,17},{17,1},{2,18},{18,2},{3,19},{19,3},{4,20},{20... | collective-permute-start | bytes 2457608 | tf_op jit(solution)/shard_map/ppermute | solution.py:65
  134.5 0.6 convolution_bitcast_fusion
  135.1 0.4 fusion.17
  135.5 0.8 collective-permute-done.1
  136.3 0.6 fusion.20
  137.0 1.1 fusion.2
  138.0 3.5 %all-to-all-start.6 = ((bf16[4,800,128]{2,1,0:T(8,128)(2,1)}), bf16[4,800,128]{2,1,0:T(8,128)(2,1)S(1)}, u32[]{:S(2)}, u32[]{:S(2)}) async-start(bf16[4,800,128]{2,1,0:T(8,128)(2,1)} %fusion.2), calls=%async_computation.6 | async-start | bytes 1638400 | tf_op jit(solution)/shard_map/all_to_all | solution.py:23
  141.5 12.3 %all-to-all-done.6 = bf16[4,800,128]{2,1,0:T(8,128)(2,1)S(1)} async-done(((bf16[4,800,128]{2,1,0:T(8,128)(2,1)}), bf16[4,800,128]{2,1,0:T(8,128)(2,1)S(1)}, u32[]{:S(2)}, u32[]{:S(2)}) %all-to-all-start.6) | async-done | bytes 819232 | tf_op jit(solution)/shard_map/all_to_all | solution.py:23
  154.5 0.7 fusion.25
  (19 shorter events, 1.8 us)
Async XLA Ops:
  0.0 6.8 %copy-start = (bf16[128,800]{0,1:T(8,128)(2,1)S(1)}, bf16[128,800]{0,1:T(8,128)(2,1)}, u32[]{:S(2)}) copy-start(bf16[128,800]{0,1:T(8,128)(2,1)} %param.1) | copy-start | bytes 614404
  2.0 24.3 %all-to-all-start = ((bf16[4,800,128]{2,1,0:T(8,128)(2,1)}), bf16[4,800,128]{2,1,0:T(8,128)(2,1)S(1)}, u32[]{:S(2)}, u32[]{:S(2)}) async-start(bf16[4,800,128]{2,1,0:T(8,128)(2,1)} %broadcast_in_dim.12), calls=%async_computation | async-start | bytes 1638400 | tf_op jit(solution)/shard_map/all_to_all | solution.py:19
  26.3 8.8 %collective-permute-start = (bf16[4,800,128]{2,1,0:T(8,128)(2,1)S(1)}, bf16[4,800,128]{2,1,0:T(8,128)(2,1)S(1)}, u32[]{:S(2)}, u32[]{:S(2)}) collective-permute-start(bf16[4,800,128]{2,1,0:T(8,128)(2,1)S(1)} %bitcast.130), channel_id=1, source_target_pairs={{0,16},{16,0},{1,17},{17,1},{2,18},{18,2},{3,19},{19,3},{4,20},{20... | collective-permute-start | bytes 2457608 | tf_op jit(solution)/shard_map/ppermute | solution.py:34
  35.2 59.7 %copy-start.1 = (bf16[4,800,128]{2,1,0:T(8,128)(2,1)}, bf16[4,800,128]{2,1,0:T(8,128)(2,1)S(1)}, u32[]{:S(2)}) copy-start(bf16[4,800,128]{2,1,0:T(8,128)(2,1)S(1)} %collective-permute-done) | copy-start | bytes 2457604
  96.8 12.5 %all-to-all-start.5 = ((bf16[4,800,128]{2,1,0:T(8,128)(2,1)}), bf16[4,800,128]{2,1,0:T(8,128)(2,1)S(1)}, u32[]{:S(2)}, u32[]{:S(2)}) async-start(bf16[4,800,128]{2,1,0:T(8,128)(2,1)} %fusion.12), calls=%async_computation.5 | async-start | bytes 1638400 | tf_op jit(solution)/shard_map/all_to_all | solution.py:23
  123.2 13.1 %collective-permute-start.1 = (bf16[4,800,128]{2,1,0:T(8,128)(2,1)S(1)}, bf16[4,800,128]{2,1,0:T(8,128)(2,1)S(1)}, u32[]{:S(2)}, u32[]{:S(2)}) collective-permute-start(bf16[4,800,128]{2,1,0:T(8,128)(2,1)S(1)} %bitcast.125), channel_id=1, source_target_pairs={{0,16},{16,0},{1,17},{17,1},{2,18},{18,2},{3,19},{19,3},{4,20},{20... | collective-permute-start | bytes 2457608 | tf_op jit(solution)/shard_map/ppermute | solution.py:65
  138.0 15.9 %all-to-all-start.6 = ((bf16[4,800,128]{2,1,0:T(8,128)(2,1)}), bf16[4,800,128]{2,1,0:T(8,128)(2,1)S(1)}, u32[]{:S(2)}, u32[]{:S(2)}) async-start(bf16[4,800,128]{2,1,0:T(8,128)(2,1)} %fusion.2), calls=%async_computation.6 | async-start | bytes 1638400 | tf_op jit(solution)/shard_map/all_to_all | solution.py:23

commit v9 on v7

--- a/solution.py
+++ b/solution.py
@@ -11,7 +11,7 @@
 coef_quintic = 2.0315
 
 SPLIT = {"yh": 4, "x": 4, "core": 2, "yl": 2, "zh": 4, "zl": 2}
-PAIRS = ("yl", "zl")
+PAIRS = ("zl", "yl")
 SWAP = [(0, 1), (1, 0)]
 
 

time: 156 us -> 156 us (level); the launches traced: 154 us -> 155 us
  blocking collectives: 105 us -> 107 us
where the time goes in v9:
time: 156 us; the launch traced here: 155 us
  blocking collectives  107 us (69%)
  starting transfers between devices  27.4 us (18%)
  waiting for transfers between devices  10.6 us (7%)
  matrix products  6.6 us (4%)
  local copies, waits for them, and re-layouts  2.38 us (2%)
  other arithmetic  1.59 us (1%)
    all_to_all x2, blocking collectives, spread(): lax.all_to_all(jnp.broadcast_to(block[None], (4,) + block.shape), axes, 0...  24.4 us
    all_gather x1, blocking collectives, on_device(): along, across = (spread(mine, 'x'), lax.all_gather(mine, 'yh'))  19.5 us
    all_to_all x1, blocking collectives, on_device(): gram = total(lax.all_to_all(total(gram), 'zh', 0, 0))  17.7 us
    all_to_all x1, blocking collectives, on_device(): gram = lax.all_to_all((gram / COLS).astype(jnp.bfloat16), PAIRS, 0, 0)  15.9 us
    all_to_all x1, blocking collectives, others(): parts = lax.all_to_all(parts, axis, 0, 0)  14.6 us
    all_gather x1, blocking collectives, on_device(): blocks = lax.all_gather(first.astype(jnp.bfloat16), 'yh')  14.4 us
    ppermute x1, starting transfers between devices, on_device(): lax.ppermute(blocks, 'core', SWAP)  11.6 us
    ppermute x1, starting transfers between devices, both_cores(): return jnp.stack([blocks, lax.ppermute(blocks, 'core', SWAP)], axis=1)  6.9 us
  transfers between devices with their start and end apart: 4, of which 3 were waited for; matrix products, arithmetic and copies ran while one was open for 1% of the time, Pallas kernels for 0%

profile of v9, /device:TPU:1, one launch (start us, length us, event | category | flops | bytes accessed | tf_op | source)
XLA Modules:
  0.0 155.3 jit_solution(13745715269316311627)
XLA Ops:
  0.0 1.9 %broadcast_in_dim.12 = bf16[4,800,128]{2,1,0:T(8,128)(2,1)} broadcast(bf16[800,128]{1,0:T(8,128)(2,1)} %bitcast.102), dimensions={1,2} | broadcast | bytes 1024000 | tf_op jit(solution)/shard_map/broadcast_in_dim | solution.py:19
  1.9 5.0 %all-to-all-start = ((bf16[4,800,128]{2,1,0:T(8,128)(2,1)}), bf16[4,800,128]{2,1,0:T(8,128)(2,1)S(1)}, u32[]{:S(2)}, u32[]{:S(2)}) async-start(bf16[4,800,128]{2,1,0:T(8,128)(2,1)} %broadcast_in_dim.12), calls=%async_computation | async-start | bytes 1638400 | tf_op jit(solution)/shard_map/all_to_all | solution.py:19
  6.9 19.5 %all-gather = bf16[3200,128]{1,0:T(8,128)(2,1)S(1)} all-gather(bf16[800,128]{1,0:T(8,128)(2,1)S(1)} %bitcast.103), channel_id=2, replica_groups=mesh['yh'=4,'x'=4,'core'=2,'yl'=2,'zh'=4,'zl'=2] {'yh'}, dimensions={0}, use_global_device_ids=true | all-gather | bytes 1024000 | tf_op jit(solution)/shard_map/all_gather | solution.py:39
  26.4 6.9 %collective-permute-start = (bf16[4,800,128]{2,1,0:T(8,128)(2,1)S(1)}, bf16[4,800,128]{2,1,0:T(8,128)(2,1)S(1)}, u32[]{:S(2)}, u32[]{:S(2)}) collective-permute-start(bf16[4,800,128]{2,1,0:T(8,128)(2,1)S(1)} %bitcast.104), channel_id=1, source_target_pairs={{0,16},{16,0},{1,17},{17,1},{2,18},{18,2},{3,19},{19,3},{4,20},{20... | collective-permute-start | bytes 2457608 | tf_op jit(solution)/shard_map/ppermute | solution.py:34
  33.3 1.9 %collective-permute-done = bf16[4,800,128]{2,1,0:T(8,128)(2,1)S(1)} collective-permute-done((bf16[4,800,128]{2,1,0:T(8,128)(2,1)S(1)}, bf16[4,800,128]{2,1,0:T(8,128)(2,1)S(1)}, u32[]{:S(2)}, u32[]{:S(2)}) %collective-permute-start) | collective-permute-done | bytes 819232 | tf_op jit(solution)/shard_map/ppermute | solution.py:34
  35.3 1.3 fusion.12
  36.6 15.9 %all_to_all.35 = bf16[4,4,128,2,128]{2,4,3,1,0:T(8,128)(2,1)S(1)} all-to-all(bf16[4,4,128,2,128]{2,4,3,1,0:T(8,128)(2,1)S(1)} %copy.14), channel_id=1, replica_groups=mesh['yh'=4,'x'=4,'core'=2,'yl'=2,'zh'=4,'zl'=2] {'zl','yl'}, dimensions={0} | all-to-all | bytes 2097152 | tf_op jit(solution)/shard_map/all_to_all | solution.py:44
  52.7 17.7 %all_to_all.36 = bf16[4,128,2,128]{1,3,2,0:T(8,128)(2,1)S(1)} all-to-all(bf16[4,128,2,128]{1,3,2,0:T(8,128)(2,1)S(1)} %reduce-precision_convert_fusion), channel_id=1, replica_groups=mesh['yh'=4,'x'=4,'core'=2,'yl'=2,'zh'=4,'zl'=2] {'zh'}, dimensions={0} | all-to-all | bytes 524288 | tf_op jit(solution)/shard_map/all_to_all | solution.py:45
  70.7 12.1 %all_to_all.37 = bf16[4,128,2,128]{3,1,2,0:T(8,128)(2,1)S(1)} all-to-all(bf16[4,128,2,128]{3,1,2,0:T(8,128)(2,1)S(1)} %broadcast_in_dim.27), channel_id=1, replica_groups=mesh['yh'=4,'x'=4,'core'=2,'yl'=2,'zh'=4,'zl'=2] {'zh'}, dimensions={0} | all-to-all | bytes 524288 | tf_op jit(solution)/shard_map/all_to_all | solution.py:19
  82.8 0.2 broadcast_in_dim.28
  83.0 12.3 %all_to_all.38 = bf16[4,4,128,2,128]{4,2,3,1,0:T(8,128)(2,1)S(1)} all-to-all(bf16[4,4,128,2,128]{4,2,3,1,0:T(8,128)(2,1)S(1)} %broadcast_in_dim.28), channel_id=1, replica_groups=mesh['yh'=4,'x'=4,'core'=2,'yl'=2,'zh'=4,'zl'=2] {'zl','yl'}, dimensions={0} | all-to-all | bytes 2097152 | tf_op jit(solution)/shard_map/all_to_all | solution.py:19
  95.3 1.9 %fusion.15 = bf16[4,800,128]{2,1,0:T(8,128)(2,1)} fusion(bf16[4,4,128,2,128]{4,2,3,1,0:T(8,128)(2,1)S(1)} %all_to_all.38, bf16[4,1,800,128]{3,2,1,0:T(8,128)(2,1)S(1)} %bitcast.112, bf16[4,1,800,128]{3,2,1,0:T(8,128)(2,1)S(1)} %bitcast.106), kind=kOutput, calls=%fused_computation.15 | convolution fusion | flops 840089600 | bytes 3506176 | tf_op jit(solution)/shard_map/dfct,edsft->ecs/dot_general | solution.py:51
  97.3 4.0 %all-to-all-start.5 = ((bf16[4,800,128]{2,1,0:T(8,128)(2,1)}), bf16[4,800,128]{2,1,0:T(8,128)(2,1)S(1)}, u32[]{:S(2)}, u32[]{:S(2)}) async-start(bf16[4,800,128]{2,1,0:T(8,128)(2,1)} %fusion.15), calls=%async_computation.5 | async-start | bytes 1638400 | tf_op jit(solution)/shard_map/all_to_all | solution.py:23
  101.2 1.7 %convolution_bitcast_fusion.1 = f32[800,128]{1,0:T(8,128)S(1)} fusion(bf16[4,1,800,128]{3,2,1,0:T(8,128)(2,1)} %bitcast.113, bf16[4,1,800,128]{3,2,1,0:T(8,128)(2,1)S(1)} %bitcast.107, bf16[4,4,128,2,128]{4,2,3,1,0:T(8,128)(2,1)S(1)} %all_to_all.38, s32[]{:T(128)S(6)} %select_n.10), kind=kOutput, calls=%fused_computation.18 | convolution fusion | flops 210534400 | bytes 2310148 | tf_op jit(solution)/shard_map/dfct,edsft->ecs/dot_general | solution.py:51
  103.0 6.8 %all-to-all-done.5 = bf16[4,800,128]{2,1,0:T(8,128)(2,1)S(1)} async-done(((bf16[4,800,128]{2,1,0:T(8,128)(2,1)}), bf16[4,800,128]{2,1,0:T(8,128)(2,1)S(1)}, u32[]{:S(2)}, u32[]{:S(2)}) %all-to-all-start.5) | async-done | bytes 819232 | tf_op jit(solution)/shard_map/all_to_all | solution.py:23
  109.8 0.3 select_reduce_fusion.1
  110.1 14.4 %all-gather.1 = bf16[3200,128]{1,0:T(8,128)(2,1)S(1)} all-gather(bf16[800,128]{1,0:T(8,128)(2,1)S(1)} %get-tuple-element.14), channel_id=3, replica_groups=mesh['yh'=4,'x'=4,'core'=2,'yl'=2,'zh'=4,'zl'=2] {'yh'}, dimensions={0}, use_global_device_ids=true | all-gather | bytes 1024000 | tf_op jit(solution)/shard_map/all_gather | solution.py:58
  124.5 11.6 %collective-permute-start.1 = (bf16[4,800,128]{2,1,0:T(8,128)(2,1)S(1)}, bf16[4,800,128]{2,1,0:T(8,128)(2,1)S(1)}, u32[]{:S(2)}, u32[]{:S(2)}) collective-permute-start(bf16[4,800,128]{2,1,0:T(8,128)(2,1)S(1)} %bitcast.108), channel_id=1, source_target_pairs={{0,16},{16,0},{1,17},{17,1},{2,18},{18,2},{3,19},{19,3},{4,20},{20... | collective-permute-start | bytes 2457608 | tf_op jit(solution)/shard_map/ppermute | solution.py:60
  136.1 1.9 %collective-permute-done.1 = bf16[4,800,128]{2,1,0:T(8,128)(2,1)S(1)} collective-permute-done((bf16[4,800,128]{2,1,0:T(8,128)(2,1)S(1)}, bf16[4,800,128]{2,1,0:T(8,128)(2,1)S(1)}, u32[]{:S(2)}, u32[]{:S(2)}) %collective-permute-start.1) | collective-permute-done | bytes 819232 | tf_op jit(solution)/shard_map/ppermute | solution.py:60
  138.0 1.0 fusion.18
  139.1 14.6 %all_to_all.39 = bf16[4,800,128]{2,1,0:T(8,128)(2,1)S(1)} all-to-all(bf16[4,800,128]{2,1,0:T(8,128)(2,1)S(1)} %fusion.18), channel_id=1, replica_groups=mesh['yh'=4,'x'=4,'core'=2,'yl'=2,'zh'=4,'zl'=2] {'x'}, dimensions={0} | all-to-all | bytes 1638400 | tf_op jit(solution)/shard_map/all_to_all | solution.py:23
  153.7 0.2 select_reduce_fusion
  154.0 0.6 fusion.22
  154.6 0.7 fusion.28
  (14 shorter events, 0.6 us)
Async XLA Ops:
  1.9 5.0 %copy-start = (bf16[128,800]{0,1:T(8,128)(2,1)S(1)}, bf16[128,800]{0,1:T(8,128)(2,1)}, u32[]{:S(2)}) copy-start(bf16[128,800]{0,1:T(8,128)(2,1)} %param.1) | copy-start | bytes 614404
  1.9 24.5 %all-to-all-start = ((bf16[4,800,128]{2,1,0:T(8,128)(2,1)}), bf16[4,800,128]{2,1,0:T(8,128)(2,1)S(1)}, u32[]{:S(2)}, u32[]{:S(2)}) async-start(bf16[4,800,128]{2,1,0:T(8,128)(2,1)} %broadcast_in_dim.12), calls=%async_computation | async-start | bytes 1638400 | tf_op jit(solution)/shard_map/all_to_all | solution.py:19
  26.4 8.8 %collective-permute-start = (bf16[4,800,128]{2,1,0:T(8,128)(2,1)S(1)}, bf16[4,800,128]{2,1,0:T(8,128)(2,1)S(1)}, u32[]{:S(2)}, u32[]{:S(2)}) collective-permute-start(bf16[4,800,128]{2,1,0:T(8,128)(2,1)S(1)} %bitcast.104), channel_id=1, source_target_pairs={{0,16},{16,0},{1,17},{17,1},{2,18},{18,2},{3,19},{19,3},{4,20},{20... | collective-permute-start | bytes 2457608 | tf_op jit(solution)/shard_map/ppermute | solution.py:34
  35.3 60.1 %copy-start.1 = (bf16[4,800,128]{2,1,0:T(8,128)(2,1)}, bf16[4,800,128]{2,1,0:T(8,128)(2,1)S(1)}, u32[]{:S(2)}) copy-start(bf16[4,800,128]{2,1,0:T(8,128)(2,1)S(1)} %collective-permute-done) | copy-start | bytes 2457604
  97.3 12.5 %all-to-all-start.5 = ((bf16[4,800,128]{2,1,0:T(8,128)(2,1)}), bf16[4,800,128]{2,1,0:T(8,128)(2,1)S(1)}, u32[]{:S(2)}, u32[]{:S(2)}) async-start(bf16[4,800,128]{2,1,0:T(8,128)(2,1)} %fusion.15), calls=%async_computation.5 | async-start | bytes 1638400 | tf_op jit(solution)/shard_map/all_to_all | solution.py:23
  124.5 13.5 %collective-permute-start.1 = (bf16[4,800,128]{2,1,0:T(8,128)(2,1)S(1)}, bf16[4,800,128]{2,1,0:T(8,128)(2,1)S(1)}, u32[]{:S(2)}, u32[]{:S(2)}) collective-permute-start(bf16[4,800,128]{2,1,0:T(8,128)(2,1)S(1)} %bitcast.108), channel_id=1, source_target_pairs={{0,16},{16,0},{1,17},{17,1},{2,18},{18,2},{3,19},{19,3},{4,20},{20... | collective-permute-start | bytes 2457608 | tf_op jit(solution)/shard_map/ppermute | solution.py:60
